TPU v7x, 256 devices: a whole 4x4x8 slice. The times are simulated.
256 devices in a mesh: context: 32 (over x, y, core), tensor: 8 (over z).
Axes of the slice: x: 4, y: 4, z: 8, core: 2. Of those that a mesh axis runs over, the one named last changes fastest.
Arguments:
- queries: bfloat16 [16384, 4096], P('context', 'tensor'), may hold values from -6 to 6
- keys: bfloat16 [16384, 4096], P('context', 'tensor'), may hold values from -6 to 6
- values: bfloat16 [16384, 4096], P('context', 'tensor'), may hold values from -6 to 6
- filters: float32 [16384, 4096], P(None, ('tensor', 'context')), may hold values from -4 to 4
- bias: float32 [4096], P(('tensor', 'context')), may hold values from -3 to 3
- out_weight: bfloat16 [4096, 4096], P(None, ('tensor', 'context')), may hold values from -0.09375 to 0.09375
Outputs:
- mixed_out: bfloat16 [16384, 4096], P('context', 'tensor')
All inputs are finite; a program needn't handle non-finite values.
Results may differ from a plain program's by a relative error of at most 0.017.
Values may be sent and summed in bfloat16 or wider, within the bound.
A program may use at most 192 MiB of HBM per device.

v0:
```python
import math

import jax
import jax.numpy as jnp
from jax import lax
from jax.sharding import PartitionSpec as P

F = 32


HIGHEST = lax.Precision.HIGHEST


def phase_table(count_rows, count_cols, modulus):
    products_grid = (
        jnp.arange(count_rows, dtype=jnp.int32)[:, None]
        * jnp.arange(count_cols, dtype=jnp.int32)[None, :]
        % modulus
    )
    angles = products_grid.astype(jnp.float32) * (2.0 * math.pi / modulus)
    return (jnp.cos(angles), jnp.sin(angles))


def outer_table(factor):
    outer_index = (
        jnp.arange(factor, dtype=jnp.int32)[:, None]
        + factor * jnp.arange(factor, dtype=jnp.int32)[None, :]
    )
    products_grid = (
        outer_index[:, :, None] * jnp.arange(factor, dtype=jnp.int32)[None, None, :] % factor**3
    )
    angles = products_grid.astype(jnp.float32) * (2.0 * math.pi / factor**3)
    return (jnp.cos(angles), jnp.sin(angles))


def block_matrix(cosines, sines, direction):
    top_row = jnp.stack([cosines, -direction * sines])
    low_row = jnp.stack([direction * sines, cosines])
    return jnp.stack([top_row, low_row])


def rotate_stacked(state, cosines, sines, direction):
    real_part = state[0]
    imag_part = state[1]
    new_real = real_part * cosines - direction * imag_part * sines
    new_imag = imag_part * cosines + direction * real_part * sines
    return jnp.stack([new_real, new_imag])


def forward_transform(signal, factor):
    half_factor = factor // 2
    channels = signal.shape[1]
    span = factor * factor * channels
    flat = signal.reshape(half_factor, span)
    first_cos, first_sin = phase_table(factor, half_factor, factor)
    first = jnp.stack([first_cos, -first_sin])
    state = jnp.einsum("rkb,bL->rkL", first, flat, precision=HIGHEST)
    state = state.reshape(2, factor, factor, factor * channels)
    inner_cos, inner_sin = phase_table(factor, factor, factor * factor)
    state = rotate_stacked(state, inner_cos[:, :, None], inner_sin[:, :, None], -1.0)
    state = state.transpose(0, 2, 1, 3).reshape(2, factor, span)
    small_cos, small_sin = phase_table(factor, factor, factor)
    forward_matrix = block_matrix(small_cos, small_sin, -1.0)
    state = jnp.einsum("rsqp,spL->rqL", forward_matrix, state, precision=HIGHEST)
    state = state.reshape(2, factor, factor, factor, channels)
    wide_cos, wide_sin = outer_table(factor)
    wide_cos = wide_cos.transpose(1, 0, 2)[:, :, :, None]
    wide_sin = wide_sin.transpose(1, 0, 2)[:, :, :, None]
    state = rotate_stacked(state, wide_cos, wide_sin, -1.0)
    state = state.transpose(0, 3, 2, 1, 4).reshape(2, factor, span)
    return jnp.einsum("rsda,saK->rdK", forward_matrix, state, precision=HIGHEST)


def inverse_transform(spectrum, factor, channels):
    half_factor = factor // 2
    span = factor * factor * channels
    small_cos, small_sin = phase_table(factor, factor, factor)
    inverse_matrix = block_matrix(small_cos, small_sin, 1.0)
    state = jnp.einsum("rsad,sdK->raK", inverse_matrix, spectrum, precision=HIGHEST)
    state = state.reshape(2, factor, factor, factor, channels)
    wide_cos, wide_sin = outer_table(factor)
    wide_cos = wide_cos.transpose(2, 0, 1)[:, :, :, None]
    wide_sin = wide_sin.transpose(2, 0, 1)[:, :, :, None]
    state = rotate_stacked(state, wide_cos, wide_sin, 1.0)
    state = state.transpose(0, 3, 1, 2, 4).reshape(2, factor, span)
    state = jnp.einsum("rspq,sqL->rpL", inverse_matrix, state, precision=HIGHEST)
    state = state.reshape(2, factor, factor, factor, channels)
    inner_cos, inner_sin = phase_table(factor, factor, factor * factor)
    state = rotate_stacked(state, inner_cos.T[:, None, :, None], inner_sin.T[:, None, :, None], 1.0)
    state = state.transpose(0, 3, 1, 2, 4).reshape(2, factor, span)
    last_cos, last_sin = phase_table(half_factor, factor, factor)
    last = jnp.stack([last_cos, -last_sin])
    result = jnp.einsum("rbk,rkL->bL", last, state, precision=HIGHEST)
    return result.reshape(half_factor * factor * factor, channels) * (1.0 / factor**3)


def body(queries, keys, values, filters, bias, out_weight):
    kv_tokens = (keys.astype(jnp.float32) * values.astype(jnp.float32)).astype(jnp.bfloat16)
    kv_channels = lax.all_to_all(kv_tokens, "context", split_axis=1, concat_axis=0, tiled=True)
    driver = lax.optimization_barrier(kv_channels).astype(jnp.float32)
    seq_length = driver.shape[0]
    channel_count = driver.shape[1]
    mean_sq = jnp.mean(filters * filters, axis=0, keepdims=True)
    scaled = filters / jnp.sqrt(seq_length * (mean_sq + 1e-06))
    drive_spec = forward_transform(driver, F)
    filter_spec = forward_transform(scaled, F)
    prod_real = drive_spec[0] * filter_spec[0] - drive_spec[1] * filter_spec[1]
    prod_imag = drive_spec[0] * filter_spec[1] + drive_spec[1] * filter_spec[0]
    convolved = inverse_transform(jnp.stack([prod_real, prod_imag]), F, channel_count)
    filtered = (convolved + bias[None, :] * driver).astype(jnp.bfloat16)
    returned = lax.all_to_all(filtered, "context", split_axis=0, concat_axis=1, tiled=True)
    gated_out = (queries.astype(jnp.float32) * returned.astype(jnp.float32)).astype(jnp.bfloat16)
    token_count = gated_out.shape[0]
    groups = lax.axis_size("tensor")
    block_rows = out_weight.shape[0] // groups
    arranged = out_weight.reshape(groups, block_rows, out_weight.shape[1]).transpose(1, 0, 2)
    my_blocks = lax.all_to_all(arranged, "tensor", split_axis=1, concat_axis=1, tiled=True)
    partial_value = jnp.einsum(
        "tr,rgc->tgc",
        gated_out,
        lax.all_gather(my_blocks, "context", axis=2, tiled=True),
        preferred_element_type=jnp.float32,
    )
    summed = lax.psum_scatter(
        partial_value.reshape(token_count, -1).astype(jnp.bfloat16),
        "tensor",
        scatter_dimension=1,
        tiled=True,
    )
    return summed


def solution(mesh):
    in_specs = (
        P("context", "tensor"),
        P("context", "tensor"),
        P("context", "tensor"),
        P(None, ("tensor", "context")),
        P(("tensor", "context")),
        P(None, ("tensor", "context")),
    )
    out_specs = P("context", "tensor")
    return jax.shard_map(body, mesh=mesh, in_specs=in_specs, out_specs=out_specs, check_vma=False)
```

profile of v0, /device:TPU:1, one launch (start us, length us, event | category | flops | bytes accessed | tf_op | source)
XLA Modules:
  0.0 482.3 jit_solution(9629823871051561027)
XLA Ops:
  6.5 1.7 copy.100
  8.2 9.0 %all-to-all-start.2 = ((bf16[512,8,16]{0,2,1:T(8,128)(2,1)}), bf16[512,8,16]{0,2,1:T(8,128)(2,1)S(1)}, u32[]{:S(2)}, u32[]{:S(2)}) async-start(bf16[512,8,16]{0,2,1:T(8,128)(2,1)} %bitcast.140), calls=%async_computation.2 | async-start | bytes 262144 | tf_op jit(solution)/shard_map/all_to_all | solution.py:117
  18.2 1.3 copy.45
  19.4 1.3 copy.46
  20.7 1.5 multiply_reduce_fusion
  22.3 4.7 copy.56
  27.0 9.2 %reshape.729 = f32[16,16384,1]{1,0,2:T(8,128)S(1)} reshape(f32[16384,16]{1,0:T(8,128)} %copy.56) | data formatting | bytes 2097152 | tf_op jit(solution)/shard_map/reshape | solution.py:54
  36.3 3.5 fusion.43
  39.7 1.6 fusion.77
  41.4 0.9 multiply_convert_fusion
  42.5 8.1 %all-to-all-start = ((bf16[512,32,16]{0,2,1:T(8,128)(2,1)}), bf16[512,32,16]{0,2,1:T(8,128)(2,1)}, u32[]{:S(2)}, u32[]{:S(2)}) async-start(bf16[512,32,16]{0,2,1:T(8,128)(2,1)} %bitcast.4), calls=%async_computation | async-start | bytes 1048576 | tf_op jit(solution)/shard_map/all_to_all | solution.py:99
  51.5 4.2 copy.95
  55.6 2.6 copy.96
  58.3 3.0 fusion.23
  61.4 2.1 fusion.22
  63.5 1.1 copy.92
  64.6 3.1 copy.48
  67.7 9.2 %reshape.724 = bf16[16,16384,1]{1,0,2:T(8,128)(2,1)S(1)} reshape(bf16[16384,16]{1,0:T(8,128)(2,1)} %copy.48) | data formatting | bytes 1048576 | tf_op jit(solution)/shard_map/reshape | solution.py:54
  76.9 1.8 fusion.44
  79.0 1.2 copy.94
  80.3 1.2 copy.93
  81.5 2.9 fusion.5
  85.2 4.4 copy.57
  89.7 5.0 %reshape.730 = f32[2,32,16384,1]{2,1,0,3:T(8,128)} reshape(f32[2,32,32,512]{3,2,1,0:T(8,128)} %copy.57) | data formatting | bytes 8388608 | tf_op jit(solution)/shard_map/reshape | solution.py:61
  94.6 5.4 %convolution_bitcast_fusion.3 = f32[2,32,16384]{2,1,0:T(8,128)S(1)} fusion(f32[2,32,16384,1]{2,1,0,3:T(8,128)} %reshape.730, f32[1,2,32,32]{3,2,1,0:T(8,128)S(1)} %get-tuple-element.34, f32[1,2,32,32]{3,2,1,0:T(8,128)S(1)} %get-tuple-element.41), kind=kOutput, calls=%fused_computation.3 | convolution fusion | flops 805310464 | bytes 8404992 | tf_op jit(solution)/shard_map/rsqp,spL->rqL/dot_general | solution.py:64
  100.1 1.6 fusion.76
  101.7 6.4 %copy.58 = f32[1,32,16384]{1,2,0:T(8,128)} copy(f32[1,32,16384]{2,1,0:T(8,128)} %get-tuple-element.28) | data formatting | bytes 4194304 | tf_op jit(solution)/shard_map/slice | solution.py:43
  108.0 4.7 copy.59
  112.7 2.8 maximum_bitcast_fusion.4
  115.5 4.4 copy.51
  119.9 5.0 %reshape.725 = f32[2,32,16384,1]{2,1,0,3:T(8,128)} reshape(f32[2,32,32,512]{3,2,1,0:T(8,128)} %copy.51) | data formatting | bytes 8388608 | tf_op jit(solution)/shard_map/reshape | solution.py:61
  124.9 5.4 %convolution_bitcast_fusion.5 = f32[2,32,16384]{2,1,0:T(8,128)S(1)} fusion(f32[2,32,16384,1]{2,1,0,3:T(8,128)} %reshape.725, f32[1,2,32,32]{3,2,1,0:T(8,128)S(1)} %get-tuple-element.34, f32[1,2,32,32]{3,2,1,0:T(8,128)S(1)} %get-tuple-element.41), kind=kOutput, calls=%fused_computation.5 | convolution fusion | flops 805310464 | bytes 8404992 | tf_op jit(solution)/shard_map/rsqp,spL->rqL/dot_general | solution.py:64
  130.3 1.6 fusion.74
  131.9 6.3 %copy.53 = f32[1,32,16384]{1,2,0:T(8,128)} copy(f32[1,32,16384]{2,1,0:T(8,128)} %get-tuple-element.23) | data formatting | bytes 4194304 | tf_op jit(solution)/shard_map/slice | solution.py:44
  138.2 4.8 copy.52
  142.9 17.7 %multiply_subtract_fusion.3 = (f32[1,32,32,32,16]{1,4,3,2,0:T(8,128)S(1)}, f32[1,32,32,32,16]{1,4,3,2,0:T(8,128)S(1)}, f32[1,32,32,32,16]{1,4,3,2,0:T(8,128)}, f32[1,32,32,32,16]{1,4,3,2,0:T(8,128)}) fusion(f32[1,32,32,32,16]{1,4,3,2,0:T(8,128)} %bitcast.153, f32[1,32,32,32,16]{1,4,3,2,0:T(8,128)} %bitcast.154, f32[32,32,32]{0,2,1:T(8,128)} %get-tuple-element.44, ...), kind=kLoop, calls=%fused_computation.19 | loop fusion | flops 6291456 | bytes 17039360 | tf_op jit(solution)/shard_map/sub | solution.py:45
  160.7 6.4 %maximum_bitcast_fusion = f32[2,32,32,32,16]{3,4,1,2,0:T(8,128)} fusion(f32[1,32,32,32,16]{1,4,3,2,0:T(8,128)S(1)} %get-tuple-element.8, f32[1,32,32,32,16]{1,4,3,2,0:T(8,128)S(1)} %get-tuple-element.7), kind=kLoop, calls=%fused_computation.8 | loop fusion | flops 1048576 | bytes 8388608 | tf_op jit(solution)/shard_map/transpose | solution.py:70
  167.0 18.8 %copy.54 = f32[2,32,32,32,16]{1,4,3,2,0:T(8,128)} copy(f32[2,32,32,32,16]{3,4,1,2,0:T(8,128)} %maximum_bitcast_fusion) | data formatting | bytes 8388608 | tf_op jit(solution)/shard_map/transpose | solution.py:70
  185.8 20.9 %convolution_bitcast_fusion.4 = f32[2,32,16384]{2,1,0:T(8,128)} fusion(f32[2,32,16384,1]{1,2,0,3:T(8,128)} %bitcast.145, f32[1,2,32,32]{3,2,1,0:T(8,128)S(1)} %get-tuple-element.34, f32[1,2,32,32]{3,2,1,0:T(8,128)S(1)} %get-tuple-element.41), kind=kOutput, calls=%fused_computation.4 | convolution fusion | flops 805310464 | bytes 8404992 | tf_op jit(solution)/shard_map/rsda,saK->rdK/dot_general | solution.py:71
  206.7 6.2 %maximum_bitcast_fusion.1 = f32[2,32,32,32,16]{3,4,1,2,0:T(8,128)} fusion(f32[1,32,32,32,16]{1,4,3,2,0:T(8,128)S(1)} %bitcast.156, f32[1,32,32,32,16]{1,4,3,2,0:T(8,128)S(1)} %bitcast.158), kind=kLoop, calls=%fused_computation.9 | loop fusion | flops 1048576 | bytes 8388608 | tf_op jit(solution)/shard_map/transpose | solution.py:70
  212.9 18.8 %copy.60 = f32[2,32,32,32,16]{1,4,3,2,0:T(8,128)} copy(f32[2,32,32,32,16]{3,4,1,2,0:T(8,128)} %maximum_bitcast_fusion.1) | data formatting | bytes 8388608 | tf_op jit(solution)/shard_map/transpose | solution.py:70
  231.7 18.3 %convolution_bitcast_fusion.2 = f32[2,32,16384]{2,1,0:T(8,128)S(1)} fusion(f32[2,32,16384,1]{1,2,0,3:T(8,128)} %bitcast.143, f32[1,2,32,32]{3,2,1,0:T(8,128)S(1)} %get-tuple-element.34, f32[1,2,32,32]{3,2,1,0:T(8,128)S(1)} %get-tuple-element.41), kind=kOutput, calls=%fused_computation.2 | convolution fusion | flops 805310464 | bytes 8404992 | tf_op jit(solution)/shard_map/rsda,saK->rdK/dot_general | solution.py:71
  250.5 3.8 convolution_bitcast_fusion.1
  254.3 1.6 fusion.73
  255.9 6.3 %copy.62 = f32[1,32,16384]{1,2,0:T(8,128)} copy(f32[1,32,16384]{2,1,0:T(8,128)} %get-tuple-element.22) | data formatting | bytes 4194304 | tf_op jit(solution)/shard_map/slice | solution.py:43
  262.2 4.6 copy.63
  266.9 7.3 %multiply_subtract_fusion.1 = (f32[1,32,32,32,16]{1,4,3,2,0:T(8,128)S(1)}, f32[1,32,32,32,16]{1,4,3,2,0:T(8,128)S(1)}) fusion(f32[1,32,32,32,16]{1,4,3,2,0:T(8,128)} %bitcast.150, f32[1,32,32,32,16]{1,4,3,2,0:T(8,128)} %bitcast.149, f32[32,32,32]{0,2,1:T(8,128)S(1)} %get-tuple-element.40, f32[32,32,32]{0,2,1:T(8,128)S(1)} %get-tuple-element.39), kind=kLoop, calls=%fused_computation.15 | loop fusion | flops 3145728 | bytes 8650752 | tf_op jit(solution)/shard_map/sub | solution.py:45
  274.2 6.1 %maximum_bitcast_fusion.2 = f32[2,32,32,32,16]{2,4,1,3,0:T(8,128)} fusion(f32[1,32,32,32,16]{1,4,3,2,0:T(8,128)S(1)} %get-tuple-element.6, f32[1,32,32,32,16]{1,4,3,2,0:T(8,128)S(1)} %get-tuple-element.5), kind=kLoop, calls=%fused_computation.10 | loop fusion | flops 1048576 | bytes 8388608 | tf_op jit(solution)/shard_map/transpose | solution.py:85
  280.2 18.8 %copy.64 = f32[2,32,32,32,16]{1,4,3,2,0:T(8,128)} copy(f32[2,32,32,32,16]{2,4,1,3,0:T(8,128)} %maximum_bitcast_fusion.2) | data formatting | bytes 8388608 | tf_op jit(solution)/shard_map/transpose | solution.py:85
  299.1 18.4 %convolution_bitcast_fusion = f32[2,32,16384]{2,1,0:T(8,128)S(1)} fusion(f32[2,32,16384,1]{1,2,0,3:T(8,128)} %bitcast.144, f32[1,2,32,32]{3,2,1,0:T(8,128)S(1)} %copy-done.11, f32[1,2,32,32]{3,2,1,0:T(8,128)S(1)} %copy-done.9), kind=kOutput, calls=%fused_computation | convolution fusion | flops 805310464 | bytes 8404992 | tf_op jit(solution)/shard_map/rspq,sqL->rpL/dot_general | solution.py:86
  317.5 1.6 fusion.72
  319.1 6.3 %copy.66 = f32[1,32,16384]{1,2,0:T(8,128)} copy(f32[1,32,16384]{2,1,0:T(8,128)} %get-tuple-element.20) | data formatting | bytes 4194304 | tf_op jit(solution)/shard_map/slice | solution.py:43
  325.4 4.6 copy.67
  330.0 7.1 %multiply_subtract_fusion = (f32[1,32,32,32,16]{1,4,3,2,0:T(8,128)S(1)}, f32[1,32,32,32,16]{1,4,3,2,0:T(8,128)S(1)}) fusion(f32[1,32,32,32,16]{1,4,3,2,0:T(8,128)} %bitcast.148, f32[1,32,32,32,16]{1,4,3,2,0:T(8,128)} %bitcast.147, f32[32,32]{0,1:T(8,128)S(1)} %copy-done.16, f32[32,32]{0,1:T(8,128)S(1)} %copy-done.13), kind=kLoop, calls=%fused_computation.13 | loop fusion | flops 3145728 | bytes 8396800 | tf_op jit(solution)/shard_map/sub | solution.py:45
  337.1 6.1 %maximum_bitcast_fusion.3 = f32[2,32,32,32,16]{2,4,1,3,0:T(8,128)} fusion(f32[1,32,32,32,16]{1,4,3,2,0:T(8,128)S(1)} %get-tuple-element.12, f32[1,32,32,32,16]{1,4,3,2,0:T(8,128)S(1)} %get-tuple-element.11), kind=kLoop, calls=%fused_computation.11 | loop fusion | flops 1048576 | bytes 8388608 | tf_op jit(solution)/shard_map/transpose | solution.py:90
  343.2 18.8 %copy.68 = f32[2,32,32,32,16]{1,4,3,2,0:T(8,128)} copy(f32[2,32,32,32,16]{2,4,1,3,0:T(8,128)} %maximum_bitcast_fusion.3) | data formatting | bytes 8388608 | tf_op jit(solution)/shard_map/transpose | solution.py:90
  362.0 16.8 %fusion = f32[16,16384]{1,0:T(8,128)S(1)} fusion(f32[2,32,16384]{1,2,0:T(8,128)} %bitcast.146, f32[1,16,32]{2,1,0:T(8,128)S(1)} %copy-done.17, f32[1,16,32]{2,1,0:T(8,128)S(1)} %copy-done.18), kind=kOutput, calls=%fused_computation.7 | convolution fusion | flops 201589760 | bytes 5246976 | tf_op jit(solution)/shard_map/rbk,rkL->bL/dot_general | solution.py:93
  378.7 5.1 %mul.1111 = f32[16384,16]{1,0:T(8,128)} reshape(f32[16,16384]{1,0:T(8,128)S(1)} %fusion) | data formatting | bytes 2097152 | tf_op jit(solution)/shard_map/mul | solution.py:94
  383.8 5.2 %copy.70 = f32[16384,16]{0,1:T(8,128)S(1)} copy(f32[16384,16]{1,0:T(8,128)} %mul.1111) | data formatting | bytes 2097152 | tf_op jit(solution)/shard_map/mul | solution.py:94
  390.1 7.4 %all-to-all-start.1 = ((bf16[32,512,16]{1,2,0:T(8,128)(2,1)}), bf16[32,512,16]{1,2,0:T(8,128)(2,1)S(1)}, u32[]{:S(2)}, u32[]{:S(2)}) async-start(bf16[32,512,16]{1,2,0:T(8,128)(2,1)} %bitcast.138), calls=%async_computation.1 | async-start | bytes 1048576 | tf_op jit(solution)/shard_map/all_to_all | solution.py:111
  397.8 11.3 %all-to-all-done.1 = bf16[32,512,16]{1,2,0:T(8,128)(2,1)S(1)} async-done(((bf16[32,512,16]{1,2,0:T(8,128)(2,1)}), bf16[32,512,16]{1,2,0:T(8,128)(2,1)S(1)}, u32[]{:S(2)}, u32[]{:S(2)}) %all-to-all-start.1) | async-done | bytes 524320 | tf_op jit(solution)/shard_map/all_to_all | solution.py:111
  409.3 6.5 %convolution_convert_fusion = bf16[512,8,512]{0,2,1:T(8,128)(2,1)} fusion(bf16[512,8,512]{0,2,1:T(8,128)(2,1)} %all-gather.2.cloned.1.call-done, bf16[512,512]{0,1:T(8,128)(2,1)S(1)} %fusion.7), kind=kOutput, calls=%fused_computation.25 | convolution fusion | flops 2149580800 | bytes 8912896 | tf_op jit(solution)/shard_map/tr,rgc->tgc/dot_general | solution.py:118
  415.8 6.4 %copy.74 = bf16[512,4096]{1,0:T(8,128)(2,1)} copy(bf16[512,4096]{0,1:T(8,128)(2,1)} %bitcast.169) | data formatting | bytes 8388608 | tf_op jit(solution)/shard_map/convert_element_type | solution.py:125
  422.2 53.1 %reduce-scatter.2.cloned.1.call-done = bf16[512,512]{1,0:T(8,128)(2,1)} async-done(((bf16[512,4096]{1,0:T(8,128)(2,1)}), bf16[512,512]{1,0:T(8,128)(2,1)}) %reduce-scatter.2.cloned.1.call-update) | async-done | bytes 524304 | tf_op jit(solution)/shard_map/reduce_scatter | solution.py:124
  (78 shorter events, 5.3 us)
Async XLA Ops:
  6.5 15.6 %copy-start.5 = (f32[16384,16]{0,1:T(8,128)S(1)}, f32[16384,16]{0,1:T(8,128)}, u32[]{:S(2)}) copy-start(f32[16384,16]{0,1:T(8,128)} %param.9) | copy-start | bytes 3145732
  8.2 34.2 %all-to-all-start.2 = ((bf16[512,8,16]{0,2,1:T(8,128)(2,1)}), bf16[512,8,16]{0,2,1:T(8,128)(2,1)S(1)}, u32[]{:S(2)}, u32[]{:S(2)}) async-start(bf16[512,8,16]{0,2,1:T(8,128)(2,1)} %bitcast.140), calls=%async_computation.2 | async-start | bytes 262144 | tf_op jit(solution)/shard_map/all_to_all | solution.py:117
  17.3 19.0 %copy-start.14 = (f32[1,32,16]{1,2,0:T(8,128)}, f32[1,32,16]{1,2,0:T(8,128)S(1)}, u32[]{:S(2)}) copy-start(f32[1,32,16]{1,2,0:T(8,128)S(1)} %get-tuple-element.46) | copy-start | bytes 6148
  18.0 40.2 %copy-start.12 = (f32[32,32]{0,1:T(8,128)}, f32[32,32]{0,1:T(8,128)S(1)}, u32[]{:S(2)}) copy-start(f32[32,32]{0,1:T(8,128)S(1)} %get-tuple-element.50) | copy-start | bytes 12292
  42.3 208.2 %copy-start.8 = (f32[1,2,32,32]{3,2,1,0:T(8,128)}, f32[1,2,32,32]{3,2,1,0:T(8,128)S(1)}, u32[]{:S(2)}) copy-start(f32[1,2,32,32]{3,2,1,0:T(8,128)S(1)} %get-tuple-element.33) | copy-start | bytes 24580
  42.3 208.2 %copy-start.10 = (f32[1,2,32,32]{3,2,1,0:T(8,128)}, f32[1,2,32,32]{3,2,1,0:T(8,128)S(1)}, u32[]{:S(2)}) copy-start(f32[1,2,32,32]{3,2,1,0:T(8,128)S(1)} %get-tuple-element.42) | copy-start | bytes 24580
  42.4 15.8 %copy-start.7 = (bf16[512,8,16]{0,2,1:T(8,128)(2,1)}, bf16[512,8,16]{0,2,1:T(8,128)(2,1)S(1)}, u32[]{:S(2)}) copy-start(bf16[512,8,16]{0,2,1:T(8,128)(2,1)S(1)} %all-to-all-done.2) | copy-start | bytes 393220
  42.5 21.1 %all-to-all-start = ((bf16[512,32,16]{0,2,1:T(8,128)(2,1)}), bf16[512,32,16]{0,2,1:T(8,128)(2,1)}, u32[]{:S(2)}, u32[]{:S(2)}) async-start(bf16[512,32,16]{0,2,1:T(8,128)(2,1)} %bitcast.4), calls=%async_computation | async-start | bytes 1048576 | tf_op jit(solution)/shard_map/all_to_all | solution.py:99
  50.6 358.7 %all-gather.2.cloned.1.call-start = ((), (), s32[]{:S(2)}) async-start(), calls=%async_computation.4 | async-start | bytes 4325376 | tf_op jit(solution)/shard_map/all_gather | solution.py:121
  64.6 12.3 %copy-start.3 = (bf16[32,2,8,512]{3,2,0,1:T(8,128)(2,1)}, bf16[32,2,8,512]{3,2,0,1:T(8,128)(2,1)S(1)}, u32[]{:S(2)}) copy-start(bf16[32,2,8,512]{3,2,0,1:T(8,128)(2,1)S(1)} %copy.92) | copy-start | bytes 1572868
  64.6 12.3 %copy-start.15 = (f32[1,32,16]{1,2,0:T(8,128)S(1)}, f32[1,32,16]{1,2,0:T(8,128)}, u32[]{:S(2)}) copy-start(f32[1,32,16]{1,2,0:T(8,128)} %copy-done.14) | copy-start | bytes 6148
  79.0 2.5 copy-start.1
  79.0 2.5 copy-start.2
  185.8 20.9 %slice-start = ((s8[8388608]{0:T(1024)(128)(4,1)}), s8[4194304]{0:T(1024)(128)(4,1)S(1)}, s32[]{:S(2)}) async-start(s8[8388608]{0:T(1024)(128)(4,1)} %bitcast.155), calls=%async_computation.6 | async-start | bytes 8388608
  185.8 20.9 %slice-start.2 = ((s8[8388608]{0:T(1024)(128)(4,1)}), s8[4194304]{0:T(1024)(128)(4,1)S(1)}, s32[]{:S(2)}) async-start(s8[8388608]{0:T(1024)(128)(4,1)} %bitcast.157), calls=%async_computation.8 | async-start | bytes 8388608
  185.8 20.9 %slice-start.1 = ((s8[8388608]{0:T(1024)(128)(4,1)}), s8[4194304]{0:T(1024)(128)(4,1)S(1)}, s32[]{:S(2)}) async-start(s8[8388608]{0:T(1024)(128)(4,1)} %bitcast.155), calls=%async_computation.7 | async-start | bytes 8388608
  185.8 20.9 %slice-start.3 = ((s8[8388608]{0:T(1024)(128)(4,1)}), s8[4194304]{0:T(1024)(128)(4,1)S(1)}, s32[]{:S(2)}) async-start(s8[8388608]{0:T(1024)(128)(4,1)} %bitcast.157), calls=%async_computation.9 | async-start | bytes 8388608
  231.7 18.4 %copy-start = (f32[2,32,16384]{2,1,0:T(8,128)S(1)}, f32[2,32,16384]{2,1,0:T(8,128)}, u32[]{:S(2)}) copy-start(f32[2,32,16384]{2,1,0:T(8,128)} %convolution_bitcast_fusion.4) | copy-start | bytes 12582916
  280.2 18.8 %copy-start.9 = (f32[1,2,32,32]{3,2,1,0:T(8,128)S(1)}, f32[1,2,32,32]{3,2,1,0:T(8,128)}, u32[]{:S(2)}) copy-start(f32[1,2,32,32]{3,2,1,0:T(8,128)} %copy-done.8) | copy-start | bytes 24580
  280.2 18.8 %copy-start.11 = (f32[1,2,32,32]{3,2,1,0:T(8,128)S(1)}, f32[1,2,32,32]{3,2,1,0:T(8,128)}, u32[]{:S(2)}) copy-start(f32[1,2,32,32]{3,2,1,0:T(8,128)} %copy-done.10) | copy-start | bytes 24580
  325.4 4.6 copy-start.13
  325.4 4.6 copy-start.16
  343.2 18.8 %copy-start.17 = (f32[1,16,32]{2,1,0:T(8,128)S(1)}, f32[1,16,32]{2,1,0:T(8,128)}, u32[]{:S(2)}) copy-start(f32[1,16,32]{2,1,0:T(8,128)} %get-tuple-element.51) | copy-start | bytes 6148
  343.2 18.8 %copy-start.18 = (f32[1,16,32]{2,1,0:T(8,128)S(1)}, f32[1,16,32]{2,1,0:T(8,128)}, u32[]{:S(2)}) copy-start(f32[1,16,32]{2,1,0:T(8,128)} %get-tuple-element.52) | copy-start | bytes 6148
  383.8 5.2 %copy-start.4 = (bf16[32,2,8,512]{3,2,0,1:T(8,128)(2,1)S(1)}, bf16[32,2,8,512]{3,2,0,1:T(8,128)(2,1)}, u32[]{:S(2)}) copy-start(bf16[32,2,8,512]{3,2,0,1:T(8,128)(2,1)} %copy-done.3) | copy-start | bytes 1572868
  383.8 5.2 %copy-start.19 = (f32[16]{0:T(128)S(1)}, f32[16]{0:T(128)}, u32[]{:S(2)}) copy-start(f32[16]{0:T(128)} %param.10) | copy-start | bytes 196
  389.0 8.5 %copy-start.6 = (bf16[512,512]{1,0:T(8,128)(2,1)S(1)}, bf16[512,512]{1,0:T(8,128)(2,1)}, u32[]{:S(2)}) copy-start(bf16[512,512]{1,0:T(8,128)(2,1)} %param.6) | copy-start | bytes 1572868
  390.1 19.0 %all-to-all-start.1 = ((bf16[32,512,16]{1,2,0:T(8,128)(2,1)}), bf16[32,512,16]{1,2,0:T(8,128)(2,1)S(1)}, u32[]{:S(2)}, u32[]{:S(2)}) async-start(bf16[32,512,16]{1,2,0:T(8,128)(2,1)} %bitcast.138), calls=%async_computation.1 | async-start | bytes 1048576 | tf_op jit(solution)/shard_map/all_to_all | solution.py:111
  397.5 77.8 %reduce-scatter.2.cloned.1.call-start = ((), (), s32[]{:S(2)}) async-start(), calls=%async_computation.5 | async-start | bytes 4718592 | tf_op jit(solution)/shard_map/reduce_scatter | solution.py:124
Sparse Core Ops, SparseCore 0:
  63.6 52.8 all-gather.1
  422.3 52.9 reduce-scatter.1
where the time goes:
time: 491 us; the launch traced here: 482 us
  local copies, waits for them, and re-layouts  205 us (42%)
  matrix products  101 us (21%)
  other arithmetic  73.5 us (15%)
  waiting for transfers between devices  64.5 us (13%)
  starting transfers between devices  24.8 us (5%)
  between operations  14.1 us (3%)
    reduce_scatter x1, waiting for transfers between devices, body(): lax.psum_scatter(partial_value.reshape(token_count, -1).astype(jnp.bfloat...  53.1 us
    dot_general x2, matrix products, forward_transform(): return jnp.einsum('rsda,saK->rdK', forward_matrix, state, precision=HIGHEST)  39.2 us
    transpose x2, local copies, waits for them, and re-layouts, inverse_transform(): state = state.transpose(0, 3, 1, 2, 4).reshape(2, factor, span)  37.6 us
    transpose x2, local copies, waits for them, and re-layouts, forward_transform(): state = state.transpose(0, 3, 2, 1, 4).reshape(2, factor, span)  37.5 us
    sub x4, other arithmetic, rotate_stacked(): new_real = real_part * cosines - direction * imag_part * sines  35.1 us
    slice x8, local copies, waits for them, and re-layouts, rotate_stacked(): imag_part = state[1]  26.6 us
    slice x6, local copies, waits for them, and re-layouts, rotate_stacked(): real_part = state[0]  25.6 us
    dot_general x1, matrix products, inverse_transform(): jnp.einsum('rspq,sqL->rpL', inverse_matrix, state, precision=HIGHEST)  18.4 us
  transfers between devices with their start and end apart: 5, of which 2 were waited for; matrix products, arithmetic and copies ran while one was open for 76% of the time, Pallas kernels for 0%

commit v1 on v0

v1 whole, which is shorter than its diff:
```python
import functools

import jax
import jax.numpy as jnp
import numpy as np
from jax import lax
from jax.experimental import pallas as pl
from jax.experimental.pallas import tpu as pltpu
from jax.sharding import PartitionSpec as P

MESH = pl.DeviceIdType.MESH
BF, F32 = jnp.bfloat16, jnp.float32
NC, NZ = 32, 8
NX, NY = 4, 4
T = 512
L = 128
CH, NG, CG = 16, 2, 8
NJ = T // L
GK = NC * CG
SEQ = L * L


def transform_tables():
    n = np.arange(L)
    a = np.exp(-2j * np.pi * np.outer(n + 0.25, n) / L)
    t = np.exp(-2j * np.pi * np.outer(n + 0.25, n) / SEQ)
    b = np.exp(-2j * np.pi * np.outer(n, n) / L)
    first = np.concatenate([a.real, a.imag], 0)
    second = np.block([[b.real, b.imag], [-b.imag, b.real]])
    second_inv = np.block([[b.real, -b.imag], [b.imag, b.real]])
    first_inv = np.concatenate([a.real.T, a.imag.T], 1)
    lane = np.arange(NC * CH)
    g, src, i = lane // GK, lane % GK // CG, lane % CG
    order = np.zeros((NC * CH, NC * CH))
    order[src * CH + g * CG + i, lane] = 1.0
    half = [jnp.asarray(x, BF) for x in (first, second, second_inv, first_inv, order)]
    return half + [jnp.asarray(x, F32) for x in (t.real, t.imag)]


def kernel(q_ref, k_ref, v_ref, filt_ref, bias_ref, w_ref, c1_ref, w2_ref, w2i_ref, c1i_ref, perm_ref, tr_ref, ti_ref,
           out_ref, stage, send1, recv1, send2, recv2, hspec, qp, gbuf, wall, acc,
           s1_sem, r1_sem, s2_sem, r2_sem, zs_sem, zr_sem, ws_sem, wr_sem):
    me = lax.axis_index("context")
    z = lax.axis_index("tensor")
    right, left = lax.rem(z + 1, NZ), lax.rem(z + NZ - 1, NZ)
    barrier = pltpu.get_barrier_semaphore()

    def greet(d, carry):
        pl.semaphore_signal(barrier, inc=1, device_id={"context": lax.rem(me + d, NC)}, device_id_type=MESH)
        return carry

    lax.fori_loop(1, NC, greet, 0)
    for side in (left, right):
        pl.semaphore_signal(barrier, inc=1, device_id={"tensor": side}, device_id_type=MESH)

    for j in range(NJ):
        rows = pl.ds(j * L, L)
        prod = (k_ref[rows, :].astype(F32) * v_ref[rows, :].astype(F32)).astype(BF).astype(F32)
        block = prod.T.reshape(NC, NG, CG, L)
        for g in range(NG):
            stage[g, :, pl.ds(j * CG, CG), :] = block[:, g]
    for g in range(NG):
        send1[g] = stage[g].astype(BF)

    pl.semaphore_wait(barrier, NC - 1 + 2)

    def exchange(src, dst, send_sem, recv_sem):
        def one(d, carry):
            peer = lax.rem(me + d, NC)
            pltpu.make_async_remote_copy(
                src_ref=src.at[peer], dst_ref=dst.at[me], send_sem=send_sem, recv_sem=recv_sem,
                device_id={"context": peer}, device_id_type=MESH).start()
            return carry

        lax.fori_loop(1, NC, one, 0)
        dst[me] = src[me]

    def exchanged(src, dst, send_sem, recv_sem):
        return pltpu.make_async_remote_copy(
            src_ref=src.at[pl.ds(0, NC - 1)], dst_ref=dst.at[pl.ds(0, NC - 1)], send_sem=send_sem, recv_sem=recv_sem,
            device_id={"context": lax.rem(me + 1, NC)}, device_id_type=MESH)

    for g in range(NG):
        exchange(send1.at[g], recv1.at[g], s1_sem.at[g], r1_sem.at[g])

    def forward(pair):
        first = jnp.dot(c1_ref[...], pair, preferred_element_type=F32)
        tr, ti = tr_ref[...], ti_ref[...]
        parts = []
        for e in range(2):
            re, im = first[:L, e * L:(e + 1) * L], first[L:, e * L:(e + 1) * L]
            parts.append(jnp.concatenate([re * tr - im * ti, re * ti + im * tr], axis=1).astype(BF))
        return jnp.dot(jnp.concatenate(parts, axis=0), w2_ref[...], preferred_element_type=F32)

    def filter_pair(i, carry):
        g, a = i // (CG // 2), lax.rem(i, CG // 2)
        taps, gains = [], []
        for e in range(2):
            tap = filt_ref[g, pl.ds(2 * a + e, L, stride=CG), :]
            mean_sq = jnp.sum(jnp.sum(tap * tap, axis=1, keepdims=True), axis=0, keepdims=True) * (1.0 / SEQ)
            gains.append((1.0 / SEQ) / jnp.sqrt(SEQ * (mean_sq + 1e-06)))
            taps.append(tap.astype(BF))
        spec = forward(jnp.concatenate(taps, axis=1))
        for e in range(2):
            hspec[i, pl.ds(e * L, L), :] = spec[e * L:(e + 1) * L] * gains[e]
        return carry

    lax.fori_loop(0, CH // 2, filter_pair, 0)
    qp[...] = jnp.dot(q_ref[...], perm_ref[...], preferred_element_type=F32).astype(BF)
    x, y, core = me // (2 * NY), lax.rem(me // 2, NY), lax.rem(me, 2)
    place = (core * 16 + x * NY + y, core * 16 + y * NX + x)
    for u in range(NZ):
        wall[u // 4, place[u // 4], u % 4] = jnp.dot(
            w_ref[:, u * NC * CH:(u + 1) * NC * CH], perm_ref[...], preferred_element_type=F32).astype(BF)

    def convolve(g):
        stage[0] = recv1[g].astype(F32)
        rows_in = stage.at[0].reshape(NC * NJ * CG, L)
        rows_out = stage.at[1].reshape(NC * NJ * CG, L)

        def pair(a, carry):
            drive = [rows_in[pl.ds(2 * a + e, L, stride=CG), :] for e in range(2)]
            spec = forward(jnp.concatenate([d.astype(BF) for d in drive], axis=1))
            h = hspec[g * (CG // 2) + a]
            ur, ui, hr, hi = spec[:, :L], spec[:, L:], h[:, :L], h[:, L:]
            prod = jnp.concatenate([ur * hr - ui * hi, ur * hi + ui * hr], axis=1).astype(BF)
            back = jnp.dot(prod, w2i_ref[...], preferred_element_type=F32)
            tr, ti = tr_ref[...], ti_ref[...]
            parts = []
            for e in range(2):
                re, im = back[e * L:(e + 1) * L, :L], back[e * L:(e + 1) * L, L:]
                parts.append(jnp.concatenate([re * tr + im * ti, im * tr - re * ti], axis=0).astype(BF))
            conv = jnp.dot(c1i_ref[...], jnp.concatenate(parts, axis=1), preferred_element_type=F32)
            for e in range(2):
                skip = bias_ref[g * CG + 2 * a + e]
                rows_out[pl.ds(2 * a + e, L, stride=CG), :] = conv[:, e * L:(e + 1) * L] + skip * drive[e]
            return carry

        lax.fori_loop(0, CG // 2, pair, 0)
        send2[g] = stage[1].astype(BF)

    for g in range(NG):
        exchanged(send1.at[g], recv1.at[g], s1_sem.at[g], r1_sem.at[g]).wait_recv()
        convolve(g)
        exchange(send2.at[g], recv2.at[g], s2_sem.at[g], r2_sem.at[g])

    hops = ((4, 3), (3, 4))

    def hop(g, way, s, j):
        slot = lax.rem(z + NZ - s, NZ) if way == 0 else lax.rem(z + s, NZ)
        return pltpu.make_async_remote_copy(
            src_ref=gbuf.at[slot, g, j], dst_ref=gbuf.at[slot, g, j],
            send_sem=zs_sem.at[g, way, s, j], recv_sem=zr_sem.at[g, way, s, j],
            device_id={"tensor": right if way == 0 else left}, device_id_type=MESH)

    for g in range(NG):
        exchanged(send2.at[g], recv2.at[g], s2_sem.at[g], r2_sem.at[g]).wait_recv()
        stage[g] = recv2[g].astype(F32)
        for j in range(NJ):
            rows = pl.ds(j * L, L)
            filtered = stage[g, :, pl.ds(j * CG, CG), :].reshape(GK, L).T
            gbuf[z, g, j] = (qp[rows, g * GK:(g + 1) * GK].astype(F32) * filtered).astype(BF)
            for way in range(2):
                hop(g, way, 0, j).start()

    def wcopy(half, start, count, sem, device):
        block = wall.at[half, pl.ds(start, count)]
        return pltpu.make_async_remote_copy(
            src_ref=block, dst_ref=block, send_sem=ws_sem.at[sem, half], recv_sem=wr_sem.at[sem, half],
            device_id={"context": device}, device_id_type=MESH)

    def along(axis, d):
        nx = lax.rem(x + d, NX) if axis == 0 else x
        ny = lax.rem(y + d, NY) if axis == 1 else y
        return (nx * NY + ny) * 2 + core

    base = (core * 16 + x * NY, core * 16 + y * NX)
    other = me + 1 - 2 * core

    def wfirst():
        for d in (1, 3, 2):
            for half in range(2):
                wcopy(half, place[half], 1, 0, along(1 - half, d)).start()

    def wsecond():
        for half in range(2):
            wcopy(half, 0, 3, 0, other).wait_recv()
        for d in (1, 3, 2):
            for half in range(2):
                wcopy(half, base[half], 4, 1, along(half, d)).start()

    def wthird():
        for half in range(2):
            wcopy(half, 0, 12, 1, other).wait_recv()
        for half in range(2):
            wcopy(half, core * 16, 16, 2, other).start()

    wfirst()
    for s in range(1, 4):
        for g in range(NG):
            for j in range(NJ):
                for way in range(2):
                    hop(g, way, s - 1, j).wait_recv()
                    if s < hops[g][way]:
                        hop(g, way, s, j).start()
            if s == 1 and g == 0:
                wsecond()
            if s == 2 and g == 1:
                wthird()
    for half in range(2):
        wcopy(half, 0, 16, 2, other).wait_recv()

    def rows_of(u, g):
        half, v = u // 4, lax.rem(u, 4)
        cols = pl.ds(g * GK, GK)
        tiles = []
        for c in range(NC):
            cx, cy, ck = c // (2 * NY), c // 2 % NY, c % 2
            a, b = ck * 16 + cx * NY + cy, ck * 16 + cy * NX + cx
            tiles.append(wall[half, jnp.where(half == 0, a, b), v, :, cols])
        return jnp.concatenate(tiles, axis=0)

    def product(u, g, left_rows):
        return lax.dot_general(left_rows, rows_of(u, g), (((1,), (1,)), ((), ())), preferred_element_type=F32)

    def add_unit(n, carry):
        u = lax.rem(z + n, NZ)
        for g in range(NG):
            acc[...] += product(u, g, gbuf[u, g].reshape(T, GK))
        return carry

    acc[...] = jnp.zeros_like(acc)
    add_unit(0, 0)
    add_unit(1, 0)
    add_unit(NZ - 1, 0)
    add_unit(2, 0)
    add_unit(NZ - 2, 0)
    add_unit(3, 0)
    add_unit(NZ - 3, 0)
    far = lax.rem(z + 4, NZ)
    for j in range(NJ):
        rows = pl.ds(j * L, L)
        hop(0, 0, 3, j).wait_recv()
        hop(1, 1, 3, j).wait_recv()
        total = acc[rows, :]
        for g in range(NG):
            total = total + product(far, g, gbuf[far, g, j])
        out_ref[rows, :] = total.astype(BF)

    for g in range(NG):
        exchanged(send1.at[g], recv1.at[g], s1_sem.at[g], r1_sem.at[g]).wait_send()
        exchanged(send2.at[g], recv2.at[g], s2_sem.at[g], r2_sem.at[g]).wait_send()
        for way in range(2):
            for s in range(hops[g][way]):
                for j in range(NJ):
                    hop(g, way, s, j).wait_send()
    for half in range(2):
        for sem, count in ((0, 3), (1, 12), (2, 16)):
            wcopy(half, 0, count, sem, other).wait_send()


def body(queries, keys, values, filters, bias, out_weight):
    taps = filters.T.reshape(NG, CG, L, L).transpose(0, 2, 1, 3).reshape(NG, L * CG, L)
    vmem = pl.BlockSpec(memory_space=pltpu.VMEM)
    smem = pl.BlockSpec(memory_space=pltpu.SMEM)
    dma = pltpu.SemaphoreType.DMA
    block = (NG, NC, NJ * CG, L)
    return pl.pallas_call(
        kernel,
        out_shape=jax.ShapeDtypeStruct((T, NC * CH), BF),
        in_specs=[vmem] * 4 + [smem] + [vmem] * 8,
        out_specs=vmem,
        scratch_shapes=[
            pltpu.VMEM(block, F32),
            pltpu.VMEM(block, BF), pltpu.VMEM(block, BF), pltpu.VMEM(block, BF), pltpu.VMEM(block, BF),
            pltpu.VMEM((CH // 2, 2 * L, 2 * L), F32),
            pltpu.VMEM((T, NC * CH), BF),
            pltpu.VMEM((NZ, NG, NJ, L, GK), BF),
            pltpu.VMEM((2, NC, 4, CH, NC * CH), BF),
            pltpu.VMEM((T, NC * CH), F32),
            dma((NG,)), dma((NG,)), dma((NG,)), dma((NG,)),
            dma((NG, 2, 4, NJ)), dma((NG, 2, 4, NJ)),
            dma((3, 2)), dma((3, 2)),
        ],
        compiler_params=pltpu.CompilerParams(
            collective_id=0, has_side_effects=True, vmem_limit_bytes=48 << 20),
    )(queries, keys, values, taps, bias, out_weight.T, *transform_tables())


def solution(mesh):
    in_specs = (
        P("context", "tensor"),
        P("context", "tensor"),
        P("context", "tensor"),
        P(None, ("tensor", "context")),
        P(("tensor", "context")),
        P(None, ("tensor", "context")),
    )
    return jax.shard_map(body, mesh=mesh, in_specs=in_specs, out_specs=P("context", "tensor"), check_vma=False)
```

time: 491 us -> 84.1 us (0.17); the launches traced: 482 us -> 83.5 us
  local copies, waits for them, and re-layouts: 205 us -> 12.9 us
  matrix products: 101 us -> 0 us
  other arithmetic: 73.5 us -> 0 us
  Pallas kernels: 0 us -> 70.6 us
  waiting for transfers between devices: 64.5 us -> 0 us
  starting transfers between devices: 24.8 us -> 0 us
  between operations: 14.1 us -> 0.02 us
    dot_general x10 -> x0, matrix products: 101 us -> none  [the longest x2 39.2 us: forward_transform(): return jnp.einsum('rsda,saK->rdK', forward_matrix, state, precision=HIGHEST)]
    transpose x6 -> x0, local copies, waits for them, and re-layouts: 84 us -> none  [the longest x2 37.6 us: inverse_transform(): state = state.transpose(0, 3, 1, 2, 4).reshape(2, factor, span)]
    pallas_call x0 -> x1, Pallas kernels: none -> 70.6 us  [body(): pl.pallas_call(kernel, out_shape=jax.ShapeDtypeStruct((T, NC * CH), BF),...]
    reduce_scatter x1 -> x0, waiting for transfers between devices: 53.1 us -> none  [body(): lax.psum_scatter(partial_value.reshape(token_count, -1).astype(jnp.bfloat...]
    slice x14 -> x0, local copies, waits for them, and re-layouts: 52.2 us -> none  [the longest x8 26.6 us: rotate_stacked(): imag_part = state[1]]
    sub x5 -> x0, other arithmetic: 35.5 us -> none  [the longest x4 35.1 us: rotate_stacked(): new_real = real_part * cosines - direction * imag_part * sines]
    reshape x5 -> x0, local copies, waits for them, and re-layouts: 30 us -> none  [the longest x2 18.4 us: forward_transform(): flat = signal.reshape(half_factor, span)]
    transpose x6 -> x0, other arithmetic: 28.3 us -> none  [the longest x2 12.6 us: forward_transform(): state = state.transpose(0, 3, 2, 1, 4).reshape(2, factor, span)]
  transfers between devices with their start and end apart: 5 -> 0, of which waited for: 2 -> 0; matrix products, arithmetic and copies ran while one was open for 76% -> 0% of each run, Pallas kernels for 0% -> 0%
where the time goes in v1:
time: 84.1 us; the launch traced here: 83.5 us
  Pallas kernels  70.6 us (84%)
  local copies, waits for them, and re-layouts  12.9 us (15%)
    pallas_call x1, Pallas kernels, body(): pl.pallas_call(kernel, out_shape=jax.ShapeDtypeStruct((T, NC * CH), BF),...  70.6 us
    unnamed x27, local copies, waits for them, and re-layouts  12.9 us

profile of v1, /device:TPU:1, one launch (start us, length us, event | category | flops | bytes accessed | tf_op | source)
XLA Modules:
  0.0 83.5 jit_solution(3658502645350944601)
XLA Ops:
  0.0 0.0 copy-start.12
  0.0 0.7 copy-done.12
  0.7 0.0 copy-start
  0.7 1.2 %copy-done = f32[16384,16]{0,1:T(8,128)S(1)} copy-done((f32[16384,16]{0,1:T(8,128)S(1)}, f32[16384,16]{0,1:T(8,128)}, u32[]{:S(2)}) %copy-start) | copy-done | bytes 1048600
  1.9 0.0 copy-start.1
  1.9 1.0 %copy-done.1 = bf16[512,512]{1,0:T(8,128)(2,1)S(1)} copy-done((bf16[512,512]{1,0:T(8,128)(2,1)S(1)}, bf16[512,512]{1,0:T(8,128)(2,1)}, u32[]{:S(2)}) %copy-start.1) | copy-done | bytes 524312
  2.9 0.0 copy-start.2
  2.9 1.0 %copy-done.2 = bf16[512,512]{1,0:T(8,128)(2,1)S(1)} copy-done((bf16[512,512]{1,0:T(8,128)(2,1)S(1)}, bf16[512,512]{1,0:T(8,128)(2,1)}, u32[]{:S(2)}) %copy-start.2) | copy-done | bytes 524312
  4.0 0.0 copy-start.3
  4.0 1.0 %copy-done.3 = bf16[512,512]{1,0:T(8,128)(2,1)S(1)} copy-done((bf16[512,512]{1,0:T(8,128)(2,1)S(1)}, bf16[512,512]{1,0:T(8,128)(2,1)}, u32[]{:S(2)}) %copy-start.3) | copy-done | bytes 524312
  5.0 0.0 copy-start.4
  5.0 1.0 %copy-done.4 = bf16[512,512]{1,0:T(8,128)(2,1)S(1)} copy-done((bf16[512,512]{1,0:T(8,128)(2,1)S(1)}, bf16[512,512]{1,0:T(8,128)(2,1)}, u32[]{:S(2)}) %copy-start.4) | copy-done | bytes 524312
  6.0 0.0 copy-start.5
  6.1 0.9 %copy-done.5 = bf16[4096,16]{0,1:T(8,128)(2,1)S(1)} copy-done((bf16[4096,16]{0,1:T(8,128)(2,1)S(1)}, bf16[4096,16]{0,1:T(8,128)(2,1)}, u32[]{:S(2)}) %copy-start.5) | copy-done | bytes 131096
  7.0 0.0 copy-start.6
  7.0 0.9 %copy-done.6 = bf16[256,256]{1,0:T(8,128)(2,1)S(1)} copy-done((bf16[256,256]{1,0:T(8,128)(2,1)S(1)}, bf16[256,256]{1,0:T(8,128)(2,1)}, u32[]{:S(2)}) %copy-start.6) | copy-done | bytes 131096
  7.9 0.0 copy-start.7
  7.9 0.9 %copy-done.7 = bf16[256,256]{1,0:T(8,128)(2,1)S(1)} copy-done((bf16[256,256]{1,0:T(8,128)(2,1)S(1)}, bf16[256,256]{1,0:T(8,128)(2,1)}, u32[]{:S(2)}) %copy-start.7) | copy-done | bytes 131096
  8.8 0.0 copy-start.8
  8.8 0.8 %copy-done.8 = f32[128,128]{1,0:T(8,128)S(1)} copy-done((f32[128,128]{1,0:T(8,128)S(1)}, f32[128,128]{1,0:T(8,128)}, u32[]{:S(2)}) %copy-start.8) | copy-done | bytes 65560
  9.6 0.0 copy-start.9
  9.6 0.8 %copy-done.9 = f32[128,128]{1,0:T(8,128)S(1)} copy-done((f32[128,128]{1,0:T(8,128)S(1)}, f32[128,128]{1,0:T(8,128)}, u32[]{:S(2)}) %copy-start.9) | copy-done | bytes 65560
  10.4 0.0 copy-start.10
  10.4 0.8 %copy-done.10 = bf16[128,256]{1,0:T(8,128)(2,1)S(1)} copy-done((bf16[128,256]{1,0:T(8,128)(2,1)S(1)}, bf16[128,256]{1,0:T(8,128)(2,1)}, u32[]{:S(2)}) %copy-start.10) | copy-done | bytes 65560
  11.3 0.0 copy-start.11
  11.3 0.8 %copy-done.11 = bf16[256,128]{1,0:T(8,128)(2,1)S(1)} copy-done((bf16[256,128]{1,0:T(8,128)(2,1)S(1)}, bf16[256,128]{1,0:T(8,128)(2,1)}, u32[]{:S(2)}) %copy-start.11) | copy-done | bytes 65560
  12.1 70.6 %shard_map.127 = bf16[512,512]{1,0:T(8,128)(2,1)S(1)} custom-call(bf16[512,512]{1,0:T(8,128)(2,1)S(1)} %copy-done.1, bf16[512,512]{1,0:T(8,128)(2,1)S(1)} %copy-done.2, bf16[512,512]{1,0:T(8,128)(2,1)S(1)} %copy-done.3, f32[2,1024,128]{2,1,0:T(8,128)S(1)} %bitcast.8, f32[16]{0:T(128)S(1)} %copy-done.12, bf16[16,4096]{1,0:T(8,128)(2,1)S(1)} %bitcast.9, ...), custom_call_target="tpu_custom_call" | custom-call | tf_op jit(solution)/shard_map/pallas_call | solution.py:268
  82.8 0.8 copy.15
Async XLA Ops:
  0.0 0.7 copy-start.12
  0.7 1.2 %copy-start = (f32[16384,16]{0,1:T(8,128)S(1)}, f32[16384,16]{0,1:T(8,128)}, u32[]{:S(2)}) copy-start(f32[16384,16]{0,1:T(8,128)} %param.16) | copy-start | bytes 3145732
  1.9 1.0 %copy-start.1 = (bf16[512,512]{1,0:T(8,128)(2,1)S(1)}, bf16[512,512]{1,0:T(8,128)(2,1)}, u32[]{:S(2)}) copy-start(bf16[512,512]{1,0:T(8,128)(2,1)} %q_ref.1) | copy-start | bytes 1572868
  2.9 1.0 %copy-start.2 = (bf16[512,512]{1,0:T(8,128)(2,1)S(1)}, bf16[512,512]{1,0:T(8,128)(2,1)}, u32[]{:S(2)}) copy-start(bf16[512,512]{1,0:T(8,128)(2,1)} %k_ref.1) | copy-start | bytes 1572868
  4.0 1.0 %copy-start.3 = (bf16[512,512]{1,0:T(8,128)(2,1)S(1)}, bf16[512,512]{1,0:T(8,128)(2,1)}, u32[]{:S(2)}) copy-start(bf16[512,512]{1,0:T(8,128)(2,1)} %v_ref.1) | copy-start | bytes 1572868
  5.0 1.0 %copy-start.4 = (bf16[512,512]{1,0:T(8,128)(2,1)S(1)}, bf16[512,512]{1,0:T(8,128)(2,1)}, u32[]{:S(2)}) copy-start(bf16[512,512]{1,0:T(8,128)(2,1)} %constant.18.clone.perm_ref) | copy-start | bytes 1572868
  6.0 0.9 %copy-start.5 = (bf16[4096,16]{0,1:T(8,128)(2,1)S(1)}, bf16[4096,16]{0,1:T(8,128)(2,1)}, u32[]{:S(2)}) copy-start(bf16[4096,16]{0,1:T(8,128)(2,1)} %param.18) | copy-start | bytes 393220
  7.0 0.9 %copy-start.6 = (bf16[256,256]{1,0:T(8,128)(2,1)S(1)}, bf16[256,256]{1,0:T(8,128)(2,1)}, u32[]{:S(2)}) copy-start(bf16[256,256]{1,0:T(8,128)(2,1)} %constant.16.clone.w2i_ref) | copy-start | bytes 393220
  7.9 0.9 %copy-start.7 = (bf16[256,256]{1,0:T(8,128)(2,1)S(1)}, bf16[256,256]{1,0:T(8,128)(2,1)}, u32[]{:S(2)}) copy-start(bf16[256,256]{1,0:T(8,128)(2,1)} %constant.15.clone.w2_ref) | copy-start | bytes 393220
  8.8 0.8 %copy-start.8 = (f32[128,128]{1,0:T(8,128)S(1)}, f32[128,128]{1,0:T(8,128)}, u32[]{:S(2)}) copy-start(f32[128,128]{1,0:T(8,128)} %constant.20.clone.ti_ref) | copy-start | bytes 196612
  9.6 0.8 %copy-start.9 = (f32[128,128]{1,0:T(8,128)S(1)}, f32[128,128]{1,0:T(8,128)}, u32[]{:S(2)}) copy-start(f32[128,128]{1,0:T(8,128)} %constant.19.clone.tr_ref) | copy-start | bytes 196612
  10.4 0.8 %copy-start.10 = (bf16[128,256]{1,0:T(8,128)(2,1)S(1)}, bf16[128,256]{1,0:T(8,128)(2,1)}, u32[]{:S(2)}) copy-start(bf16[128,256]{1,0:T(8,128)(2,1)} %constant.17.clone.c1i_ref) | copy-start | bytes 196612
  11.3 0.8 %copy-start.11 = (bf16[256,128]{1,0:T(8,128)(2,1)S(1)}, bf16[256,128]{1,0:T(8,128)(2,1)}, u32[]{:S(2)}) copy-start(bf16[256,128]{1,0:T(8,128)(2,1)} %constant.14.clone.c1_ref) | copy-start | bytes 196612

commit v2 on v1

v2 whole, which is shorter than its diff:
```python
import functools

import jax
import jax.numpy as jnp
import numpy as np
from jax import lax
from jax.experimental import pallas as pl
from jax.experimental.pallas import tpu as pltpu
from jax.sharding import PartitionSpec as P

MESH = pl.DeviceIdType.MESH
BF, F32 = jnp.bfloat16, jnp.float32
NC, NZ = 32, 8
NX, NY = 4, 4
T = 512
L = 128
CH, NG, CG = 16, 4, 4
NJ = T // L
NP = 2
GK = NC * CG
SEQ = L * L
FAR_FIRST = sorted(((dx, dy, dc) for dx in range(NX) for dy in range(NY) for dc in range(2) if dx or dy or dc),
                   key=lambda d: -(min(d[0], NX - d[0]) + min(d[1], NY - d[1])))


def transform_tables():
    n = np.arange(L)
    a = np.exp(-2j * np.pi * np.outer(n + 0.25, n) / L)
    t = np.exp(-2j * np.pi * np.outer(n + 0.25, n) / SEQ)
    b = np.exp(-2j * np.pi * np.outer(n, n) / L)
    first = np.concatenate([a.real, a.imag], 0)
    second = np.block([[b.real, b.imag], [-b.imag, b.real]])
    second_inv = np.block([[b.real, -b.imag], [b.imag, b.real]])
    first_inv = np.concatenate([a.real.T, a.imag.T], 1)
    lane = np.arange(NC * CH)
    g, i, src = lane // GK, lane % GK // NC, lane % NC
    order = np.zeros((NC * CH, NC * CH))
    order[src * CH + g * CG + i, lane] = 1.0
    half = [jnp.asarray(x, BF) for x in (first, second, second_inv, first_inv, order)]
    return half + [jnp.asarray(x, F32) for x in (t.real, t.imag)]


def kernel(*refs):
    operands, out_ref, copies, scratch = refs[:13], refs[13], refs[14:27], refs[27:]
    q_ref, k_ref, v_ref, filt_ref, bias_ref, w_ref, c1_ref, w2_ref, w2i_ref, c1i_ref, perm_ref, tr_ref, ti_ref = copies
    (in_sem, turned, stage, send1, recv1, send2, recv2, hspec, qp, gbuf, wall, acc,
     s1_sem, r1_sem, s2_sem, r2_sem, zs_sem, zr_sem, ws_sem, wr_sem) = scratch
    me = lax.axis_index("context")
    z = lax.axis_index("tensor")
    x, y, core = me // (2 * NY), lax.rem(me // 2, NY), lax.rem(me, 2)
    right, left = lax.rem(z + 1, NZ), lax.rem(z + NZ - 1, NZ)
    barrier = pltpu.get_barrier_semaphore()

    def load(n):
        return pltpu.make_async_copy(operands[n], copies[n], in_sem.at[n])

    def arrived(*numbers):
        for n in numbers:
            load(n).wait()

    def greet(d, carry):
        pl.semaphore_signal(barrier, inc=1, device_id={"context": lax.rem(me + d, NC)}, device_id_type=MESH)
        return carry

    load(1).start()
    load(2).start()
    lax.fori_loop(1, NC, greet, 0)
    for side in (left, right):
        pl.semaphore_signal(barrier, inc=1, device_id={"tensor": side}, device_id_type=MESH)
    for n in (3, 6, 7, 11, 12, 10, 0, 5, 8, 9, 4):
        load(n).start()

    arrived(1, 2)
    for j in range(NJ):
        rows = pl.ds(j * L, L)
        prod = (k_ref[rows, :].astype(F32) * v_ref[rows, :].astype(F32)).astype(BF).astype(F32)
        turned[j] = prod.T

    def gather_rows(ref, first):
        return ref[pl.ds(first, NC, stride=CH), :]

    for g in range(NG):
        to = stage.at[g % 2]
        for j in range(NJ):
            for i in range(CG):
                to[pl.ds(j * CG + i, NC, stride=NJ * CG), :] = gather_rows(turned.at[j], g * CG + i)
        send1[g] = to[...].astype(BF).reshape(NC, NJ * CG, L)

    pl.semaphore_wait(barrier, NC - 1 + 2)

    def exchange(src, dst, send_sem, recv_sem):
        for dx, dy, dc in FAR_FIRST:
            peer = (lax.rem(x + dx, NX) * NY + lax.rem(y + dy, NY)) * 2 + lax.rem(core + dc, 2)
            pltpu.make_async_remote_copy(
                src_ref=src.at[peer], dst_ref=dst.at[me], send_sem=send_sem, recv_sem=recv_sem,
                device_id={"context": peer}, device_id_type=MESH).start()
        dst[me] = src[me]

    def exchanged(src, dst, send_sem, recv_sem):
        return pltpu.make_async_remote_copy(
            src_ref=src.at[pl.ds(0, NC - 1)], dst_ref=dst.at[pl.ds(0, NC - 1)], send_sem=send_sem, recv_sem=recv_sem,
            device_id={"context": lax.rem(me + 1, NC)}, device_id_type=MESH)

    def drive(g):
        return send1.at[g], recv1.at[g], s1_sem.at[g], r1_sem.at[g]

    def answer(g):
        return send2.at[g], recv2.at[g], s2_sem.at[g], r2_sem.at[g]

    exchange(*drive(0))
    exchange(*drive(1))
    exchange(*drive(2))
    exchange(*drive(3))

    def forward(blocks):
        first = jnp.dot(c1_ref[...], jnp.concatenate(blocks, axis=1), preferred_element_type=F32)
        tr, ti = tr_ref[...], ti_ref[...]
        parts = []
        for e in range(CG):
            re, im = first[:L, e * L:(e + 1) * L], first[L:, e * L:(e + 1) * L]
            parts.append(jnp.concatenate([re * tr - im * ti, re * ti + im * tr], axis=1).astype(BF))
        return jnp.dot(jnp.concatenate(parts, axis=0), w2_ref[...], preferred_element_type=F32)

    arrived(3, 6, 7, 11, 12)

    def filter_chunk(g, carry):
        taps, gains = [], []
        for e in range(CG):
            tap = filt_ref[g // 2, pl.ds(lax.rem(g, 2) * CG + e, L, stride=2 * CG), :]
            mean_sq = jnp.sum(jnp.sum(tap * tap, axis=1, keepdims=True), axis=0, keepdims=True) * (1.0 / SEQ)
            gains.append((1.0 / SEQ) / jnp.sqrt(SEQ * (mean_sq + 1e-06)))
            taps.append(tap.astype(BF))
        spec = forward(taps)
        for e in range(CG):
            hspec[g, pl.ds(e * L, L), :] = spec[e * L:(e + 1) * L] * gains[e]
        return carry

    lax.fori_loop(0, NG, filter_chunk, 0)
    arrived(0, 10, 5)
    qp[...] = jnp.dot(q_ref[...], perm_ref[...], preferred_element_type=F32).astype(BF)
    place = (core * 16 + x * NY + y, core * 16 + y * NX + x)
    for u in range(NZ):
        wall[u // 4, place[u // 4], u % 4] = jnp.dot(
            w_ref[:, u * NC * CH:(u + 1) * NC * CH], perm_ref[...], preferred_element_type=F32).astype(BF)
    arrived(8, 9, 4)

    def convolve(g):
        exchanged(*drive(g)).wait_recv()
        rows_in, rows_out = stage.at[0], stage.at[1]
        rows_in[...] = recv1[g].astype(F32).reshape(NC * NJ * CG, L)
        own = [rows_in[pl.ds(e, L, stride=CG), :] for e in range(CG)]
        spec = forward([d.astype(BF) for d in own])
        h = hspec[g]
        ur, ui, hr, hi = spec[:, :L], spec[:, L:], h[:, :L], h[:, L:]
        prod = jnp.concatenate([ur * hr - ui * hi, ur * hi + ui * hr], axis=1).astype(BF)
        back = jnp.dot(prod, w2i_ref[...], preferred_element_type=F32)
        tr, ti = tr_ref[...], ti_ref[...]
        parts = []
        for e in range(CG):
            re, im = back[e * L:(e + 1) * L, :L], back[e * L:(e + 1) * L, L:]
            parts.append(jnp.concatenate([re * tr + im * ti, im * tr - re * ti], axis=0).astype(BF))
        conv = jnp.dot(c1i_ref[...], jnp.concatenate(parts, axis=1), preferred_element_type=F32)
        for e in range(CG):
            skip = bias_ref[g * CG + e]
            rows_out[pl.ds(e, L, stride=CG), :] = conv[:, e * L:(e + 1) * L] + skip * own[e]
        send2[g] = rows_out[...].astype(BF).reshape(NC, NJ * CG, L)

    def hops(g, way):
        return 4 - (g + way) % 2

    def hop(g, way, s, p):
        slot = lax.rem(z + NZ - s, NZ) if way == 0 else lax.rem(z + s, NZ)
        block = gbuf.at[slot, g, pl.ds(p * NJ // NP, NJ // NP)]
        return pltpu.make_async_remote_copy(
            src_ref=block, dst_ref=block, send_sem=zs_sem.at[g, way, s, p], recv_sem=zr_sem.at[g, way, s, p],
            device_id={"tensor": right if way == 0 else left}, device_id_type=MESH)

    def gate(g):
        exchanged(*answer(g)).wait_recv()
        got = stage.at[0]
        got[...] = recv2[g].astype(F32).reshape(NC * NJ * CG, L)
        for j in range(NJ):
            filtered = jnp.concatenate([gather_rows(got, j * CG + e) for e in range(CG)], axis=0).T
            gbuf[z, g, j] = (qp[j * L:(j + 1) * L, g * GK:(g + 1) * GK].astype(F32) * filtered).astype(BF)
            if (j + 1) % (NJ // NP) == 0:
                for way in range(2):
                    hop(g, way, 0, j // (NJ // NP)).start()

    def forward_hop(g, s):
        for p in range(NP):
            for way in range(2):
                hop(g, way, s - 1, p).wait_recv()
                if s < hops(g, way):
                    hop(g, way, s, p).start()

    def wcopy(half, start, count, sem, device):
        block = wall.at[half, pl.ds(start, count)]
        return pltpu.make_async_remote_copy(
            src_ref=block, dst_ref=block, send_sem=ws_sem.at[sem, half], recv_sem=wr_sem.at[sem, half],
            device_id={"context": device}, device_id_type=MESH)

    def along(axis, d):
        nx = lax.rem(x + d, NX) if axis == 0 else x
        ny = lax.rem(y + d, NY) if axis == 1 else y
        return (nx * NY + ny) * 2 + core

    base = (core * 16 + x * NY, core * 16 + y * NX)
    other = me + 1 - 2 * core

    def wfirst():
        for d in (1, 3, 2):
            for half in range(2):
                wcopy(half, place[half], 1, 0, along(1 - half, d)).start()

    def wsecond():
        for half in range(2):
            wcopy(half, 0, 3, 0, other).wait_recv()
        for d in (1, 3, 2):
            for half in range(2):
                wcopy(half, base[half], 4, 1, along(half, d)).start()

    def wthird():
        for half in range(2):
            wcopy(half, 0, 12, 1, other).wait_recv()
        for half in range(2):
            wcopy(half, core * 16, 16, 2, other).start()

    def wlast():
        for half in range(2):
            wcopy(half, 0, 16, 2, other).wait_recv()

    def rows_of(u, cols):
        half, v = u // 4, lax.rem(u, 4)
        tiles = []
        for c in range(NC):
            cx, cy, ck = c // (2 * NY), c // 2 % NY, c % 2
            a, b = ck * 16 + cx * NY + cy, ck * 16 + cy * NX + cx
            tiles.append(wall[half, jnp.where(half == 0, a, b), v, :, cols])
        return jnp.concatenate(tiles, axis=0)

    def product(u, first, count, rows):
        left_rows = jnp.concatenate([gbuf[u, g, rows].reshape(-1, GK) for g in range(first, first + count)], axis=1)
        return lax.dot_general(left_rows, rows_of(u, pl.ds(first * GK, count * GK)), (((1,), (1,)), ((), ())),
                               preferred_element_type=F32)

    def add_unit(n, carry):
        acc[...] += product(lax.rem(z + n, NZ), 0, NG, pl.ds(0, NJ))
        return carry

    convolve(0)
    exchange(*answer(0))
    convolve(1)
    exchange(*answer(1))
    convolve(2)
    exchange(*answer(2))
    convolve(3)
    exchange(*answer(3))
    gate(0)
    gate(1)
    forward_hop(0, 1)
    gate(2)
    forward_hop(1, 1)
    forward_hop(0, 2)
    gate(3)
    wfirst()
    forward_hop(2, 1)
    wsecond()
    forward_hop(1, 2)
    forward_hop(0, 3)
    forward_hop(3, 1)
    forward_hop(2, 2)
    forward_hop(1, 3)
    wthird()
    forward_hop(3, 2)
    wlast()
    acc[...] = product(z, 0, NG, pl.ds(0, NJ))
    for n in (1, NZ - 1, 2, NZ - 2):
        add_unit(n, 0)
    forward_hop(2, 3)
    forward_hop(3, 3)
    for n in (3, NZ - 3):
        add_unit(n, 0)
    far = lax.rem(z + 4, NZ)
    for g in range(NG):
        if g == 2:
            acc[...] += product(far, 0, 2, pl.ds(0, NJ))
        for p in range(NP):
            if g < 2:
                hop(g, g % 2, 3, p).wait_recv()
    for p in range(NP):
        for g in (2, 3):
            hop(g, g % 2, 3, p).wait_recv()
        width = NJ // NP
        rows = pl.ds(p * width * L, width * L)
        out_ref[rows, :] = (acc[rows, :] + product(far, 2, 2, pl.ds(p * width, width))).astype(BF)

    for g in range(NG):
        exchanged(*drive(g)).wait_send()
        exchanged(*answer(g)).wait_send()
        for way in range(2):
            for s in range(hops(g, way)):
                for p in range(NP):
                    hop(g, way, s, p).wait_send()
    for half in range(2):
        for sem, count in ((0, 3), (1, 12), (2, 16)):
            wcopy(half, 0, count, sem, other).wait_send()


def body(queries, keys, values, filters, bias, out_weight):
    taps = filters.T.reshape(2, CH // 2, L, L).transpose(0, 2, 1, 3).reshape(2, L * CH // 2, L)
    vmem = pl.BlockSpec(memory_space=pltpu.VMEM)
    dma = pltpu.SemaphoreType.DMA
    block = (NG, NC, NJ * CG, L)
    operands = (queries, keys, values, taps, bias, out_weight.T, *transform_tables())
    return pl.pallas_call(
        kernel,
        out_shape=jax.ShapeDtypeStruct((T, NC * CH), BF),
        in_specs=[pl.BlockSpec(memory_space=pl.ANY)] * len(operands),
        out_specs=vmem,
        scratch_shapes=[
            *[(pltpu.SMEM if n == 4 else pltpu.VMEM)(x.shape, x.dtype) for n, x in enumerate(operands)],
            dma((len(operands),)),
            pltpu.VMEM((NJ, NC * CH, L), F32),
            pltpu.VMEM((2, NC * NJ * CG, L), F32),
            pltpu.VMEM(block, BF), pltpu.VMEM(block, BF), pltpu.VMEM(block, BF), pltpu.VMEM(block, BF),
            pltpu.VMEM((NG, CG * L, 2 * L), F32),
            pltpu.VMEM((T, NC * CH), BF),
            pltpu.VMEM((NZ, NG, NJ, L, GK), BF),
            pltpu.VMEM((2, NC, 4, CH, NC * CH), BF),
            pltpu.VMEM((T, NC * CH), F32),
            dma((NG,)), dma((NG,)), dma((NG,)), dma((NG,)),
            dma((NG, 2, 4, NP)), dma((NG, 2, 4, NP)),
            dma((3, 2)), dma((3, 2)),
        ],
        compiler_params=pltpu.CompilerParams(
            collective_id=0, has_side_effects=True, vmem_limit_bytes=56 << 20),
    )(*operands)


def solution(mesh):
    in_specs = (
        P("context", "tensor"),
        P("context", "tensor"),
        P("context", "tensor"),
        P(None, ("tensor", "context")),
        P(("tensor", "context")),
        P(None, ("tensor", "context")),
    )
    return jax.shard_map(body, mesh=mesh, in_specs=in_specs, out_specs=P("context", "tensor"), check_vma=False)
```

time: 84.1 us -> 68.1 us (0.81)
  local copies, waits for them, and re-layouts: 12.9 us -> 1.87 us
  Pallas kernels: 70.6 us -> 66.1 us
    unnamed x27 -> x1, local copies, waits for them, and re-layouts: 12.9 us -> 1.87 us
    pallas_call x1, Pallas kernels: 70.6 us -> 66.1 us  [body(): pl.pallas_call(kernel, out_shape=jax.ShapeDtypeStruct((T, NC * CH), BF),...]
where the time goes in v2:
time: 68.1 us; the launch traced here: 67.9 us
  Pallas kernels  66.1 us (97%)
  local copies, waits for them, and re-layouts  1.87 us (3%)
    pallas_call x1, Pallas kernels, body(): pl.pallas_call(kernel, out_shape=jax.ShapeDtypeStruct((T, NC * CH), BF),...  66.1 us
    unnamed x1, local copies, waits for them, and re-layouts  1.87 us

profile of v2, /device:TPU:1, one launch (start us, length us, event | category | flops | bytes accessed | tf_op | source)
XLA Modules:
  0.0 67.9 jit_solution(15352274245835312307)
XLA Ops:
  0.0 66.1 %shard_map.127 = bf16[512,512]{1,0:T(8,128)(2,1)} custom-call(bf16[512,512]{1,0:T(8,128)(2,1)} %refs_0_.1, bf16[512,512]{1,0:T(8,128)(2,1)} %refs_1_.1, bf16[512,512]{1,0:T(8,128)(2,1)} %refs_2_.1, f32[2,1024,128]{2,1,0:T(8,128)} %bitcast.8, f32[16]{0:T(128)} %refs_4_.1, bf16[16,4096]{1,0:T(8,128)(2,1)} %bitcast.9, bf16[256,128]{1,0:T(8,128)(2,1)} %constant.14.clone.refs_6_, ...), custom_call_target="tpu_custom_call" | custom-call | tf_op jit(solution)/shard_map/pallas_call | solution.py:315
  66.1 1.9 %copy.15 = bf16[512,512]{1,0:T(8,128)(2,1)} copy(bf16[512,512]{1,0:T(8,128)(2,1)} %shard_map.127) | data formatting | bytes 1048576

commit v3 on v2

--- a/solution.py
+++ b/solution.py
@@ -16,8 +16,8 @@
 L = 128
 CH, NG, CG = 16, 4, 4
 NJ = T // L
-NP = 2
 GK = NC * CG
+TWIN = (3, 2)
 SEQ = L * L
 FAR_FIRST = sorted(((dx, dy, dc) for dx in range(NX) for dy in range(NY) for dc in range(2) if dx or dy or dc),
                    key=lambda d: -(min(d[0], NX - d[0]) + min(d[1], NY - d[1])))
@@ -44,7 +44,8 @@
     operands, out_ref, copies, scratch = refs[:13], refs[13], refs[14:27], refs[27:]
     q_ref, k_ref, v_ref, filt_ref, bias_ref, w_ref, c1_ref, w2_ref, w2i_ref, c1i_ref, perm_ref, tr_ref, ti_ref = copies
     (in_sem, turned, stage, send1, recv1, send2, recv2, hspec, qp, gbuf, wall, acc,
-     s1_sem, r1_sem, s2_sem, r2_sem, zs_sem, zr_sem, ws_sem, wr_sem) = scratch
+     taps_out, taps_in, twin_q, twin_drive, send3, recv3,
+     s1_sem, r1_sem, s2_sem, r2_sem, zs_sem, zr_sem, ws_sem, wr_sem, ts_sem, tr_sem, s3_sem, r3_sem) = scratch
     me = lax.axis_index("context")
     z = lax.axis_index("tensor")
     x, y, core = me // (2 * NY), lax.rem(me // 2, NY), lax.rem(me, 2)
@@ -121,7 +122,28 @@
             parts.append(jnp.concatenate([re * tr - im * ti, re * ti + im * tr], axis=1).astype(BF))
         return jnp.dot(jnp.concatenate(parts, axis=0), w2_ref[...], preferred_element_type=F32)
 
-    arrived(3, 6, 7, 11, 12)
+    def twin(kind, way):
+        g = TWIN[way]
+        src = (taps_out.at[way], qp.at[g], recv1.at[g])[kind]
+        dst = (taps_in, twin_q, twin_drive)[kind].at[way]
+        return pltpu.make_async_remote_copy(
+            src_ref=src, dst_ref=dst, send_sem=ts_sem.at[kind, way], recv_sem=tr_sem.at[kind, way],
+            device_id={"tensor": right if way == 0 else left}, device_id_type=MESH)
+
+    arrived(3, 6, 7, 11, 12, 4)
+    row = lax.broadcasted_iota(jnp.int32, (2 * CG * 2, L), 0)
+    for way in range(2):
+        g = TWIN[way]
+        tail = jnp.zeros((2 * CG * 2, L), F32)
+        for e in range(CG):
+            tap = filt_ref[g // 2, pl.ds(g % 2 * CG + e, L, stride=2 * CG), :]
+            mean_sq = jnp.sum(jnp.sum(tap * tap, axis=1, keepdims=True), axis=0, keepdims=True) * (1.0 / SEQ)
+            taps_out[way, e * L:(e + 1) * L, :] = (tap / jnp.sqrt(SEQ * (mean_sq + 1e-06))).astype(BF)
+            skip = jnp.full((2 * CG * 2, L), bias_ref[g * CG + e], F32)
+            tail = jnp.where(row == e, skip, tail)
+            tail = jnp.where(row == CG + e, skip - skip.astype(BF).astype(F32), tail)
+        taps_out[way, CG * L:, :] = tail.astype(BF)
+        twin(0, way).start()
 
     def filter_chunk(g, carry):
         taps, gains = [], []
@@ -137,20 +159,21 @@
 
     lax.fori_loop(0, NG, filter_chunk, 0)
     arrived(0, 10, 5)
-    qp[...] = jnp.dot(q_ref[...], perm_ref[...], preferred_element_type=F32).astype(BF)
+    for g in (3, 2, 0, 1):
+        qp[g] = jnp.dot(q_ref[...], perm_ref[:, g * GK:(g + 1) * GK], preferred_element_type=F32).astype(BF)
+        if g in TWIN:
+            twin(1, TWIN.index(g)).start()
     place = (core * 16 + x * NY + y, core * 16 + y * NX + x)
     for u in range(NZ):
         wall[u // 4, place[u // 4], u % 4] = jnp.dot(
             w_ref[:, u * NC * CH:(u + 1) * NC * CH], perm_ref[...], preferred_element_type=F32).astype(BF)
-    arrived(8, 9, 4)
-
-    def convolve(g):
-        exchanged(*drive(g)).wait_recv()
+    arrived(8, 9)
+
+    def transform(source, h, skips, target):
         rows_in, rows_out = stage.at[0], stage.at[1]
-        rows_in[...] = recv1[g].astype(F32).reshape(NC * NJ * CG, L)
+        rows_in[...] = source.astype(F32).reshape(NC * NJ * CG, L)
         own = [rows_in[pl.ds(e, L, stride=CG), :] for e in range(CG)]
         spec = forward([d.astype(BF) for d in own])
-        h = hspec[g]
         ur, ui, hr, hi = spec[:, :L], spec[:, L:], h[:, :L], h[:, L:]
         prod = jnp.concatenate([ur * hr - ui * hi, ur * hi + ui * hr], axis=1).astype(BF)
         back = jnp.dot(prod, w2i_ref[...], preferred_element_type=F32)
@@ -161,37 +184,62 @@
             parts.append(jnp.concatenate([re * tr + im * ti, im * tr - re * ti], axis=0).astype(BF))
         conv = jnp.dot(c1i_ref[...], jnp.concatenate(parts, axis=1), preferred_element_type=F32)
         for e in range(CG):
-            skip = bias_ref[g * CG + e]
-            rows_out[pl.ds(e, L, stride=CG), :] = conv[:, e * L:(e + 1) * L] + skip * own[e]
-        send2[g] = rows_out[...].astype(BF).reshape(NC, NJ * CG, L)
+            rows_out[pl.ds(e, L, stride=CG), :] = conv[:, e * L:(e + 1) * L] + skips[e] * own[e]
+        target[...] = rows_out[...].astype(BF).reshape(NC, NJ * CG, L)
+
+    def convolve(g):
+        exchanged(*drive(g)).wait_recv()
+        if g in TWIN:
+            twin(2, TWIN.index(g)).start()
+        transform(recv1[g], hspec[g], [bias_ref[g * CG + e] for e in range(CG)], send2.at[g])
+
+    def twin_answer(way):
+        return send3.at[way], recv3.at[way], s3_sem.at[way], r3_sem.at[way]
+
+    def convolve_twin(way):
+        twin(0, way).wait_recv()
+        h = forward([taps_in[way, e * L:(e + 1) * L, :] for e in range(CG)]) * (1.0 / SEQ)
+        tail = taps_in[way, CG * L:, :].astype(F32)
+        twin(2, way).wait_recv()
+        transform(twin_drive[way], h, [tail[e:e + 1] + tail[CG + e:CG + e + 1] for e in range(CG)], send3.at[way])
+        exchange(*twin_answer(way))
 
     def hops(g, way):
-        return 4 - (g + way) % 2
-
-    def hop(g, way, s, p):
-        slot = lax.rem(z + NZ - s, NZ) if way == 0 else lax.rem(z + s, NZ)
-        block = gbuf.at[slot, g, pl.ds(p * NJ // NP, NJ // NP)]
+        return 4 if g == way else 3
+
+    def hop(g, way, s):
+        s_slot = s + (1 if TWIN[way] == g else 0)
+        slot = lax.rem(z + NZ - s_slot, NZ) if way == 0 else lax.rem(z + s_slot, NZ)
+        block = gbuf.at[slot, g]
         return pltpu.make_async_remote_copy(
-            src_ref=block, dst_ref=block, send_sem=zs_sem.at[g, way, s, p], recv_sem=zr_sem.at[g, way, s, p],
+            src_ref=block, dst_ref=block, send_sem=zs_sem.at[g, way, s], recv_sem=zr_sem.at[g, way, s],
             device_id={"tensor": right if way == 0 else left}, device_id_type=MESH)
+
+    def gate_block(source, queries, g, slot):
+        got = stage.at[0]
+        got[...] = source.astype(F32).reshape(NC * NJ * CG, L)
+        for j in range(NJ):
+            filtered = jnp.concatenate([gather_rows(got, j * CG + e) for e in range(CG)], axis=0).T
+            gbuf[slot, g, j] = (queries[j * L:(j + 1) * L, :].astype(F32) * filtered).astype(BF)
 
     def gate(g):
         exchanged(*answer(g)).wait_recv()
-        got = stage.at[0]
-        got[...] = recv2[g].astype(F32).reshape(NC * NJ * CG, L)
-        for j in range(NJ):
-            filtered = jnp.concatenate([gather_rows(got, j * CG + e) for e in range(CG)], axis=0).T
-            gbuf[z, g, j] = (qp[j * L:(j + 1) * L, g * GK:(g + 1) * GK].astype(F32) * filtered).astype(BF)
-            if (j + 1) % (NJ // NP) == 0:
-                for way in range(2):
-                    hop(g, way, 0, j // (NJ // NP)).start()
-
-    def forward_hop(g, s):
-        for p in range(NP):
-            for way in range(2):
-                hop(g, way, s - 1, p).wait_recv()
-                if s < hops(g, way):
-                    hop(g, way, s, p).start()
+        gate_block(recv2[g], qp.at[g], g, z)
+        for way in range(2):
+            if TWIN[way] != g:
+                hop(g, way, 0).start()
+
+    def gate_twin(way):
+        exchanged(*twin_answer(way)).wait_recv()
+        twin(1, way).wait_recv()
+        gate_block(recv3[way], twin_q.at[way], TWIN[way], left if way == 0 else right)
+        hop(TWIN[way], way, 0).start()
+
+    def forward_hop(g, s, ways=(0, 1)):
+        for way in ways:
+            hop(g, way, s - 1).wait_recv()
+            if s < hops(g, way):
+                hop(g, way, s).start()
 
     def wcopy(half, start, count, sem, device):
         block = wall.at[half, pl.ds(start, count)]
@@ -238,14 +286,13 @@
             tiles.append(wall[half, jnp.where(half == 0, a, b), v, :, cols])
         return jnp.concatenate(tiles, axis=0)
 
-    def product(u, first, count, rows):
-        left_rows = jnp.concatenate([gbuf[u, g, rows].reshape(-1, GK) for g in range(first, first + count)], axis=1)
-        return lax.dot_general(left_rows, rows_of(u, pl.ds(first * GK, count * GK)), (((1,), (1,)), ((), ())),
-                               preferred_element_type=F32)
-
-    def add_unit(n, carry):
-        acc[...] += product(lax.rem(z + n, NZ), 0, NG, pl.ds(0, NJ))
-        return carry
+    def product(blocks):
+        left_rows = jnp.concatenate([gbuf[u, g].reshape(T, GK) for u, g in blocks], axis=1)
+        right_rows = jnp.concatenate([rows_of(u, pl.ds(g * GK, GK)) for u, g in blocks], axis=1)
+        return lax.dot_general(left_rows, right_rows, (((1,), (1,)), ((), ())), preferred_element_type=F32)
+
+    def unit(n):
+        return lax.rem(z + n, NZ)
 
     convolve(0)
     exchange(*answer(0))
@@ -257,50 +304,54 @@
     exchange(*answer(3))
     gate(0)
     gate(1)
+    convolve_twin(1)
+    convolve_twin(0)
     forward_hop(0, 1)
     gate(2)
+    gate(3)
     forward_hop(1, 1)
     forward_hop(0, 2)
-    gate(3)
+    gate_twin(1)
+    gate_twin(0)
     wfirst()
-    forward_hop(2, 1)
+    forward_hop(2, 1, (0,))
+    forward_hop(3, 1, (1,))
+    forward_hop(1, 2)
     wsecond()
-    forward_hop(1, 2)
     forward_hop(0, 3)
-    forward_hop(3, 1)
-    forward_hop(2, 2)
+    forward_hop(3, 1, (0,))
+    forward_hop(2, 1, (1,))
     forward_hop(1, 3)
+    forward_hop(2, 2, (0,))
+    forward_hop(3, 2, (1,))
     wthird()
-    forward_hop(3, 2)
+    forward_hop(3, 2, (0,))
+    forward_hop(2, 2, (1,))
     wlast()
-    acc[...] = product(z, 0, NG, pl.ds(0, NJ))
+    acc[...] = product([(z, g) for g in range(NG)])
     for n in (1, NZ - 1, 2, NZ - 2):
-        add_unit(n, 0)
+        acc[...] += product([(unit(n), g) for g in range(NG)])
+    third, fifth, far = unit(3), unit(NZ - 3), unit(4)
+    acc[...] += product([(third, 0), (third, 1), (third, 2)])
+    acc[...] += product([(fifth, 0), (fifth, 1), (fifth, 3)])
+    for g in range(2):
+        hop(g, g, 3).wait_recv()
+    acc[...] += product([(far, 0), (far, 1)])
     forward_hop(2, 3)
+    acc[...] += product([(fifth, 2), (far, 2)])
     forward_hop(3, 3)
-    for n in (3, NZ - 3):
-        add_unit(n, 0)
-    far = lax.rem(z + 4, NZ)
-    for g in range(NG):
-        if g == 2:
-            acc[...] += product(far, 0, 2, pl.ds(0, NJ))
-        for p in range(NP):
-            if g < 2:
-                hop(g, g % 2, 3, p).wait_recv()
-    for p in range(NP):
-        for g in (2, 3):
-            hop(g, g % 2, 3, p).wait_recv()
-        width = NJ // NP
-        rows = pl.ds(p * width * L, width * L)
-        out_ref[rows, :] = (acc[rows, :] + product(far, 2, 2, pl.ds(p * width, width))).astype(BF)
+    out_ref[...] = (acc[...] + product([(third, 3), (far, 3)])).astype(BF)
 
     for g in range(NG):
         exchanged(*drive(g)).wait_send()
         exchanged(*answer(g)).wait_send()
         for way in range(2):
             for s in range(hops(g, way)):
-                for p in range(NP):
-                    hop(g, way, s, p).wait_send()
+                hop(g, way, s).wait_send()
+    for way in range(2):
+        exchanged(*twin_answer(way)).wait_send()
+        for kind in range(3):
+            twin(kind, way).wait_send()
     for half in range(2):
         for sem, count in ((0, 3), (1, 12), (2, 16)):
             wcopy(half, 0, count, sem, other).wait_send()
@@ -324,13 +375,16 @@
             pltpu.VMEM((2, NC * NJ * CG, L), F32),
             pltpu.VMEM(block, BF), pltpu.VMEM(block, BF), pltpu.VMEM(block, BF), pltpu.VMEM(block, BF),
             pltpu.VMEM((NG, CG * L, 2 * L), F32),
-            pltpu.VMEM((T, NC * CH), BF),
+            pltpu.VMEM((NG, T, GK), BF),
             pltpu.VMEM((NZ, NG, NJ, L, GK), BF),
             pltpu.VMEM((2, NC, 4, CH, NC * CH), BF),
             pltpu.VMEM((T, NC * CH), F32),
+            pltpu.VMEM((2, CG * L + 4 * CG, L), BF), pltpu.VMEM((2, CG * L + 4 * CG, L), BF),
+            pltpu.VMEM((2, T, GK), BF),
+            *[pltpu.VMEM((2, NC, NJ * CG, L), BF)] * 3,
             dma((NG,)), dma((NG,)), dma((NG,)), dma((NG,)),
-            dma((NG, 2, 4, NP)), dma((NG, 2, 4, NP)),
-            dma((3, 2)), dma((3, 2)),
+            dma((NG, 2, 4)), dma((NG, 2, 4)),
+            dma((3, 2)), dma((3, 2)), dma((3, 2)), dma((3, 2)), dma((2,)), dma((2,)),
         ],
         compiler_params=pltpu.CompilerParams(
             collective_id=0, has_side_effects=True, vmem_limit_bytes=56 << 20),

time: 68.1 us -> 64.9 us (0.953)
  Pallas kernels: 66.1 us -> 62.9 us
    pallas_call x1, Pallas kernels: 66.1 us -> 62.9 us  [body(): pl.pallas_call(kernel, out_shape=jax.ShapeDtypeStruct((T, NC * CH), BF),...]
where the time goes in v3:
time: 64.9 us; the launch traced here: 64.8 us
  Pallas kernels  62.9 us (97%)
  local copies, waits for them, and re-layouts  1.87 us (3%)
    pallas_call x1, Pallas kernels, body(): pl.pallas_call(kernel, out_shape=jax.ShapeDtypeStruct((T, NC * CH), BF),...  62.9 us
    unnamed x1, local copies, waits for them, and re-layouts  1.87 us

profile of v3, /device:TPU:1, one launch (start us, length us, event | category | flops | bytes accessed | tf_op | source)
XLA Modules:
  0.0 64.8 jit_solution(5907566230344149283)
XLA Ops:
  0.0 62.9 %shard_map.127 = bf16[512,512]{1,0:T(8,128)(2,1)} custom-call(bf16[512,512]{1,0:T(8,128)(2,1)} %refs_0_.1, bf16[512,512]{1,0:T(8,128)(2,1)} %refs_1_.1, bf16[512,512]{1,0:T(8,128)(2,1)} %refs_2_.1, f32[2,1024,128]{2,1,0:T(8,128)} %bitcast.8, f32[16]{0:T(128)} %refs_4_.1, bf16[16,4096]{1,0:T(8,128)(2,1)} %bitcast.9, bf16[256,128]{1,0:T(8,128)(2,1)} %constant.14.clone.refs_6_, ...), custom_call_target="tpu_custom_call" | custom-call | tf_op jit(solution)/shard_map/pallas_call | solution.py:366
  62.9 1.9 %copy.15 = bf16[512,512]{1,0:T(8,128)(2,1)} copy(bf16[512,512]{1,0:T(8,128)(2,1)} %shard_map.127) | data formatting | bytes 1048576

commit v4 on v3

--- a/solution.py
+++ b/solution.py
@@ -365,7 +365,7 @@
     operands = (queries, keys, values, taps, bias, out_weight.T, *transform_tables())
     return pl.pallas_call(
         kernel,
-        out_shape=jax.ShapeDtypeStruct((T, NC * CH), BF),
+        out_shape=pltpu.VMEM((T, NC * CH), BF),
         in_specs=[pl.BlockSpec(memory_space=pl.ANY)] * len(operands),
         out_specs=vmem,
         scratch_shapes=[

time: 64.9 us -> 63 us (0.971)
  local copies, waits for them, and re-layouts: 1.87 us -> 0.8 us
  Pallas kernels: 62.9 us -> 62.1 us
    unnamed x1, local copies, waits for them, and re-layouts: 1.87 us -> 0.8 us
    pallas_call x1, Pallas kernels: 62.9 us -> 62.1 us  [body(): pl.pallas_call(kernel, out_shape=pltpu.VMEM((T, NC * CH), BF), in_specs=[...]
where the time goes in v4:
time: 63 us; the launch traced here: 62.9 us
  Pallas kernels  62.1 us (99%)
  local copies, waits for them, and re-layouts  0.8 us (1%)
    pallas_call x1, Pallas kernels, body(): pl.pallas_call(kernel, out_shape=pltpu.VMEM((T, NC * CH), BF), in_specs=[...  62.1 us

profile of v4, /device:TPU:1, one launch (start us, length us, event | category | flops | bytes accessed | tf_op | source)
XLA Modules:
  0.0 62.9 jit_solution(1380585609611094456)
XLA Ops:
  0.0 62.1 %shard_map.127 = bf16[512,512]{1,0:T(8,128)(2,1)S(1)} custom-call(bf16[512,512]{1,0:T(8,128)(2,1)} %refs_0_.1, bf16[512,512]{1,0:T(8,128)(2,1)} %refs_1_.1, bf16[512,512]{1,0:T(8,128)(2,1)} %refs_2_.1, f32[2,1024,128]{2,1,0:T(8,128)} %bitcast.8, f32[16]{0:T(128)} %refs_4_.1, bf16[16,4096]{1,0:T(8,128)(2,1)} %bitcast.9, ...), custom_call_target="tpu_custom_call" | custom-call | tf_op jit(solution)/shard_map/pallas_call | solution.py:366
  62.1 0.8 %copy.15 = bf16[512,512]{1,0:T(8,128)(2,1)} copy(bf16[512,512]{1,0:T(8,128)(2,1)S(1)} %shard_map.127) | data formatting | bytes 1048576

commit v5 on v4

--- a/solution.py
+++ b/solution.py
@@ -59,13 +59,11 @@
         for n in numbers:
             load(n).wait()
 
-    def greet(d, carry):
-        pl.semaphore_signal(barrier, inc=1, device_id={"context": lax.rem(me + d, NC)}, device_id_type=MESH)
-        return carry
-
     load(1).start()
     load(2).start()
-    lax.fori_loop(1, NC, greet, 0)
+    for dx, dy, dc in FAR_FIRST:
+        peer = (lax.rem(x + dx, NX) * NY + lax.rem(y + dy, NY)) * 2 + lax.rem(core + dc, 2)
+        pl.semaphore_signal(barrier, inc=1, device_id={"context": peer}, device_id_type=MESH)
     for side in (left, right):
         pl.semaphore_signal(barrier, inc=1, device_id={"tensor": side}, device_id_type=MESH)
     for n in (3, 6, 7, 11, 12, 10, 0, 5, 8, 9, 4):
@@ -79,15 +77,6 @@
 
     def gather_rows(ref, first):
         return ref[pl.ds(first, NC, stride=CH), :]
-
-    for g in range(NG):
-        to = stage.at[g % 2]
-        for j in range(NJ):
-            for i in range(CG):
-                to[pl.ds(j * CG + i, NC, stride=NJ * CG), :] = gather_rows(turned.at[j], g * CG + i)
-        send1[g] = to[...].astype(BF).reshape(NC, NJ * CG, L)
-
-    pl.semaphore_wait(barrier, NC - 1 + 2)
 
     def exchange(src, dst, send_sem, recv_sem):
         for dx, dy, dc in FAR_FIRST:
@@ -108,10 +97,15 @@
     def answer(g):
         return send2.at[g], recv2.at[g], s2_sem.at[g], r2_sem.at[g]
 
-    exchange(*drive(0))
-    exchange(*drive(1))
-    exchange(*drive(2))
-    exchange(*drive(3))
+    for g in range(NG):
+        to = stage.at[g % 2]
+        for j in range(NJ):
+            for i in range(CG):
+                to[pl.ds(j * CG + i, NC, stride=NJ * CG), :] = gather_rows(turned.at[j], g * CG + i)
+        send1[g] = to[...].astype(BF).reshape(NC, NJ * CG, L)
+        if g == 0:
+            pl.semaphore_wait(barrier, NC - 1 + 2)
+        exchange(*drive(g))
 
     def forward(blocks):
         first = jnp.dot(c1_ref[...], jnp.concatenate(blocks, axis=1), preferred_element_type=F32)
@@ -337,10 +331,12 @@
     for g in range(2):
         hop(g, g, 3).wait_recv()
     acc[...] += product([(far, 0), (far, 1)])
-    forward_hop(2, 3)
-    acc[...] += product([(fifth, 2), (far, 2)])
-    forward_hop(3, 3)
-    out_ref[...] = (acc[...] + product([(third, 3), (far, 3)])).astype(BF)
+    hop(2, 0, 2).wait_recv()
+    hop(3, 1, 2).wait_recv()
+    acc[...] += product([(fifth, 2), (third, 3)])
+    hop(2, 1, 2).wait_recv()
+    hop(3, 0, 2).wait_recv()
+    out_ref[...] = (acc[...] + product([(far, 2), (far, 3)])).astype(BF)
 
     for g in range(NG):
         exchanged(*drive(g)).wait_send()

time: 63 us -> 62.9 us (level)
  no operation moved by 1% of the time
where the time goes in v5:
time: 62.9 us; the launch traced here: 62.8 us
  Pallas kernels  62 us (99%)
  local copies, waits for them, and re-layouts  0.8 us (1%)
    pallas_call x1, Pallas kernels, body(): pl.pallas_call(kernel, out_shape=pltpu.VMEM((T, NC * CH), BF), in_specs=[...  62 us

profile of v5, /device:TPU:1, one launch (start us, length us, event | category | flops | bytes accessed | tf_op | source)
XLA Modules:
  0.0 62.8 jit_solution(13270967923794296830)
XLA Ops:
  0.0 62.0 %shard_map.127 = bf16[512,512]{1,0:T(8,128)(2,1)S(1)} custom-call(bf16[512,512]{1,0:T(8,128)(2,1)} %refs_0_.1, bf16[512,512]{1,0:T(8,128)(2,1)} %refs_1_.1, bf16[512,512]{1,0:T(8,128)(2,1)} %refs_2_.1, f32[2,1024,128]{2,1,0:T(8,128)} %bitcast.8, f32[16]{0:T(128)} %refs_4_.1, bf16[16,4096]{1,0:T(8,128)(2,1)} %bitcast.9, ...), custom_call_target="tpu_custom_call" | custom-call | tf_op jit(solution)/shard_map/pallas_call | solution.py:362
  62.0 0.8 %copy.15 = bf16[512,512]{1,0:T(8,128)(2,1)} copy(bf16[512,512]{1,0:T(8,128)(2,1)S(1)} %shard_map.127) | data formatting | bytes 1048576

commit v6 on v5

--- a/solution.py
+++ b/solution.py
@@ -66,8 +66,6 @@
         pl.semaphore_signal(barrier, inc=1, device_id={"context": peer}, device_id_type=MESH)
     for side in (left, right):
         pl.semaphore_signal(barrier, inc=1, device_id={"tensor": side}, device_id_type=MESH)
-    for n in (3, 6, 7, 11, 12, 10, 0, 5, 8, 9, 4):
-        load(n).start()
 
     arrived(1, 2)
     for j in range(NJ):
@@ -106,6 +104,9 @@
         if g == 0:
             pl.semaphore_wait(barrier, NC - 1 + 2)
         exchange(*drive(g))
+        if g == 0:
+            for n in (3, 6, 7, 11, 12, 10, 0, 5, 8, 9, 4):
+                load(n).start()
 
     def forward(blocks):
         first = jnp.dot(c1_ref[...], jnp.concatenate(blocks, axis=1), preferred_element_type=F32)

time: 62.9 us -> 63.5 us (level)
  no operation moved by 1% of the time
where the time goes in v6:
time: 63.5 us; the launch traced here: 63.3 us
  Pallas kernels  62.5 us (98%)
  local copies, waits for them, and re-layouts  0.8 us (1%)
    pallas_call x1, Pallas kernels, body(): pl.pallas_call(kernel, out_shape=pltpu.VMEM((T, NC * CH), BF), in_specs=[...  62.5 us

profile of v6, /device:TPU:1, one launch (start us, length us, event | category | flops | bytes accessed | tf_op | source)
XLA Modules:
  0.0 63.3 jit_solution(2306530060838825084)
XLA Ops:
  0.0 62.5 %shard_map.127 = bf16[512,512]{1,0:T(8,128)(2,1)S(1)} custom-call(bf16[512,512]{1,0:T(8,128)(2,1)} %refs_0_.1, bf16[512,512]{1,0:T(8,128)(2,1)} %refs_1_.1, bf16[512,512]{1,0:T(8,128)(2,1)} %refs_2_.1, f32[2,1024,128]{2,1,0:T(8,128)} %bitcast.8, f32[16]{0:T(128)} %refs_4_.1, bf16[16,4096]{1,0:T(8,128)(2,1)} %bitcast.9, ...), custom_call_target="tpu_custom_call" | custom-call | tf_op jit(solution)/shard_map/pallas_call | solution.py:363
  62.5 0.8 %copy.15 = bf16[512,512]{1,0:T(8,128)(2,1)} copy(bf16[512,512]{1,0:T(8,128)(2,1)S(1)} %shard_map.127) | data formatting | bytes 1048576
